TPU v7x, 32 devices: a whole 2x2x4 slice. The times are simulated.
32 devices in a mesh: dp: 8 (over z, y), tensor: 4 (over x, core).
Axes of the slice: x: 2, y: 2, z: 4, core: 2. Of those that a mesh axis runs over, the one named last changes fastest.
Arguments:
- patches: bfloat16 [24576, 384], P(('dp', 'tensor')), may hold values from -6 to 6
- classes: bfloat16 [96, 384], P(('dp', 'tensor')), may hold values from -6 to 6
- group_size: int32 [32], P(('dp', 'tensor')), may hold values from 196 to 576, as said below
- image_count: int32 [32], P(('dp', 'tensor')), may hold values from 1 to 3, as said below
- self_entry: bfloat16 [384, 1152], P('dp', 'tensor'), may hold values from -0.3125 to 0.3125
- self_exit: bfloat16 [384, 384], P('dp', 'tensor'), may hold values from -1.25 to 1.25
- self_expand: bfloat16 [384, 1536], P('dp', 'tensor'), may hold values from -0.3125 to 0.3125
- self_reduce: bfloat16 [1536, 384], P('tensor', 'dp'), may hold values from -0.15625 to 0.15625
- self_vectors: float32 [10, 384], replicated, may hold values from -0.75 to 1.625
- self_talking: float32 [17, 8], replicated, may hold values from -0.7 to 1.9
- self_offset: float32 [1536], replicated, may hold values from -1.5 to 1.5
- class_entry: bfloat16 [384, 1152], P('dp', 'tensor'), may hold values from -0.3125 to 0.3125
- class_exit: bfloat16 [384, 384], P('dp', 'tensor'), may hold values from -1.25 to 1.25
- class_expand: bfloat16 [384, 1536], P('dp', 'tensor'), may hold values from -0.3125 to 0.3125
- class_reduce: bfloat16 [1536, 384], P('tensor', 'dp'), may hold values from -0.15625 to 0.15625
- class_vectors: float32 [10, 384], replicated, may hold values from -0.75 to 1.625
- class_offset: float32 [1536], replicated, may hold values from -1.5 to 1.5
- patch_cotangent: bfloat16 [24576, 384], P(('dp', 'tensor')), may hold values from -6 to 6
- class_cotangent: bfloat16 [96, 384], P(('dp', 'tensor')), may hold values from -6 to 6
Outputs:
- patch_result: bfloat16 [24576, 384], P(('dp', 'tensor'))
- class_result: bfloat16 [96, 384], P(('dp', 'tensor'))
- patch_grad: float32 [24576, 384], P(('dp', 'tensor'))
- class_grad: float32 [96, 384], P(('dp', 'tensor'))
- grad_self_entry: float32 [384, 1152], P('dp', 'tensor')
- grad_self_exit: float32 [384, 384], P('dp', 'tensor')
- grad_self_expand: float32 [384, 1536], P('dp', 'tensor')
- grad_self_reduce: float32 [1536, 384], P('tensor', 'dp')
- grad_self_vectors: float32 [10, 384], replicated
- grad_self_talking: float32 [17, 8], replicated
- grad_self_offset: float32 [1536], replicated
- grad_class_entry: float32 [384, 1152], P('dp', 'tensor')
- grad_class_exit: float32 [384, 384], P('dp', 'tensor')
- grad_class_expand: float32 [384, 1536], P('dp', 'tensor')
- grad_class_reduce: float32 [1536, 384], P('tensor', 'dp')
- grad_class_vectors: float32 [10, 384], replicated
- grad_class_offset: float32 [1536], replicated
Inputs may be any that keep to these rules, and one draw needn't show every extreme that they name: `group_size`: each device holds images of one size only. `image_count`: images fill a device's first rows in order, image j on rows j * s to (j + 1) * s - 1 for its image size s; at most 768 // s images, and the rows after them are padding.
All inputs are finite; a program needn't handle non-finite values.
Results may differ from a plain program's by a relative error of at most 0.018.
Values may be sent and summed in bfloat16 or wider, within the bound.
A program may use at most 256 MiB of HBM per device.

v0:
```python
import jax
import jax.numpy as jnp
from jax import lax
from jax.sharding import PartitionSpec as P

HEADS = 8
FF = 1536


EPSILON = 1e-06
NEGATIVE = -1e30
HIGH = lax.Precision.HIGHEST
ROOT_HALF = 0.7071067811865476
ROOT_TWO_PI = 2.5066282746310002


def contract(left, right, left_dim, right_dim):
    return lax.dot_general(
        left, right, (((left_dim,), (right_dim,)), ((), ())), preferred_element_type=jnp.float32
    )


def normalize(rows, gain, shift):
    mean = jnp.mean(rows, -1, keepdims=True)
    centered = rows - mean
    inverse = lax.rsqrt(jnp.mean(centered * centered, -1, keepdims=True) + EPSILON)
    unit = centered * inverse
    return (unit * gain + shift, (unit, inverse))


def normalize_back(grad, gain, saved):
    unit, inverse = saved
    scaled = grad * gain
    inner = jnp.mean(scaled * unit, -1, keepdims=True)
    result = inverse * (scaled - jnp.mean(scaled, -1, keepdims=True) - unit * inner)
    return (result, jnp.sum(grad * unit, 0), jnp.sum(grad, 0))


def smooth(hidden):
    return 0.5 * hidden * (1.0 + lax.erf(hidden * ROOT_HALF))


def smooth_slope(hidden):
    return (
        0.5 * (1.0 + lax.erf(hidden * ROOT_HALF))
        + hidden * jnp.exp(-0.5 * hidden * hidden) / ROOT_TWO_PI
    )


def feed_forward(rows, vectors, expand, reduce_value, offset):
    normed, saved = normalize(rows, vectors[6], vectors[7])
    normed_low = normed.astype(jnp.bfloat16)
    gathered = lax.all_gather(normed_low, "tensor", axis=0, tiled=True)
    hidden = jnp.dot(gathered, expand, preferred_element_type=jnp.float32) + offset
    active = smooth(hidden).astype(jnp.bfloat16)
    summed = lax.psum_scatter(
        jnp.dot(active, reduce_value, preferred_element_type=jnp.float32).astype(jnp.bfloat16),
        "tensor",
        scatter_dimension=0,
        tiled=True,
    ).astype(jnp.float32)
    branch = summed + vectors[8]
    return (rows + vectors[9] * branch, (saved, gathered, hidden, active, branch))


def feed_back(grad, cache, vectors, expand, reduce_value):
    saved, gathered, hidden, active, branch = cache
    grad_scale = jnp.sum(grad * branch, 0)
    delta = (vectors[9] * grad).astype(jnp.bfloat16)
    grad_bias = jnp.sum(delta, 0, dtype=jnp.float32)
    deltas = lax.all_gather(delta, "tensor", axis=0, tiled=True)
    grad_reduce = contract(active, deltas, 0, 0)
    grad_hidden = (contract(deltas, reduce_value, 1, 1) * smooth_slope(hidden)).astype(jnp.bfloat16)
    grad_offset = jnp.sum(grad_hidden, 0, dtype=jnp.float32)
    grad_expand = contract(gathered, grad_hidden, 0, 0)
    grad_normed = lax.psum_scatter(
        contract(grad_hidden, expand, 1, 1).astype(jnp.bfloat16),
        "tensor",
        scatter_dimension=0,
        tiled=True,
    ).astype(jnp.float32)
    grad_rows, grad_gain, grad_shift = normalize_back(grad_normed, vectors[6], saved)
    return (
        grad + grad_rows,
        (grad_gain, grad_shift, grad_bias, grad_scale),
        grad_offset,
        grad_expand,
        grad_reduce,
    )


def score_block(query_block, keys_all, mask_block, mix_pre, scale):
    scores = (
        jnp.einsum("bhe,khe->hbk", query_block, keys_all, preferred_element_type=jnp.float32)
        * scale
    )
    mixed = jnp.einsum("gh,hbk->gbk", mix_pre, scores, precision=HIGH)
    return (scores, jnp.where(mask_block[None], mixed, NEGATIVE))


def post_weights(probs, mix_post, post_bias, mask_block):
    posted = jnp.einsum("gh,hbk->gbk", mix_post, probs, precision=HIGH) + post_bias[:, None, None]
    return jnp.where(mask_block[None], posted, 0.0).astype(jnp.bfloat16)


def self_forward(rows, vectors, entry, exit_weight, talking, allowed):
    count, width = rows.shape
    heads = talking.shape[1]
    depth = width // heads
    scale = depth ** (-0.5)
    normed, saved = normalize(rows, vectors[0], vectors[1])
    normed_low = normed.astype(jnp.bfloat16)
    bias = jnp.concatenate([vectors[2], jnp.zeros((width,), jnp.float32), vectors[3]])
    triple = (jnp.dot(normed_low, entry, preferred_element_type=jnp.float32) + bias).astype(
        jnp.bfloat16
    )
    split = triple.reshape(count, 3, heads, depth)
    keys_all, values_all = (split[:, 1], split[:, 2])
    block = 768
    queries = split[:, 0].reshape(count // block, block, heads, depth)
    masks = allowed.reshape(count // block, block, count)
    mix_pre, mix_post, post_bias = (talking[:heads], talking[heads : 2 * heads], talking[2 * heads])

    def forward_block(item):
        query_block, mask_block = item
        scores, mixed = score_block(query_block, keys_all, mask_block, mix_pre, scale)
        top = jnp.max(mixed, -1, keepdims=True)
        raised = jnp.exp(mixed - top)
        total = jnp.sum(raised, -1, keepdims=True)
        weights = post_weights(raised / total, mix_post, post_bias, mask_block)
        out = jnp.einsum("hbk,khe->bhe", weights, values_all, preferred_element_type=jnp.float32)
        return (out.astype(jnp.bfloat16), (top + jnp.log(total))[..., 0])

    attended, log_total = lax.map(forward_block, (queries, masks))
    attended = attended.reshape(count, width)
    branch = jnp.dot(attended, exit_weight, preferred_element_type=jnp.float32) + vectors[4]
    cache = (saved, normed_low, split, queries, masks, log_total, attended, branch)
    return (rows + vectors[5] * branch, cache)


def self_back(grad, cache, vectors, entry, exit_weight, talking):
    saved, normed_low, split, queries, masks, log_total, attended, branch = cache
    count, width = grad.shape
    heads = talking.shape[1]
    depth = width // heads
    scale = depth ** (-0.5)
    keys_all, values_all = (split[:, 1], split[:, 2])
    mix_pre, mix_post, post_bias = (talking[:heads], talking[heads : 2 * heads], talking[2 * heads])
    grad_scale = jnp.sum(grad * branch, 0)
    delta = (vectors[5] * grad).astype(jnp.bfloat16)
    grad_bias = jnp.sum(delta, 0, dtype=jnp.float32)
    grad_exit = contract(attended, delta, 0, 0)
    grad_out = contract(delta, exit_weight, 1, 1).astype(jnp.bfloat16).reshape(queries.shape)

    def back_block(carry, item):
        grad_keys, grad_values, grad_pre, grad_post, grad_shift = carry
        query_block, mask_block, total_block, out_block = item
        scores, mixed = score_block(query_block, keys_all, mask_block, mix_pre, scale)
        probs = jnp.exp(mixed - total_block[..., None])
        weights = post_weights(probs, mix_post, post_bias, mask_block)
        grad_weights = jnp.where(
            mask_block[None],
            jnp.einsum("bhe,khe->hbk", out_block, values_all, preferred_element_type=jnp.float32),
            0.0,
        )
        grad_values = grad_values + jnp.einsum(
            "hbk,bhe->khe", weights, out_block, preferred_element_type=jnp.float32
        )
        grad_shift = grad_shift + jnp.sum(grad_weights, (1, 2))
        grad_post = grad_post + jnp.einsum("gbk,hbk->gh", grad_weights, probs, precision=HIGH)
        grad_probs = jnp.einsum("gh,gbk->hbk", mix_post, grad_weights, precision=HIGH)
        grad_mixed = probs * (grad_probs - jnp.sum(grad_probs * probs, -1, keepdims=True))
        grad_pre = grad_pre + jnp.einsum("gbk,hbk->gh", grad_mixed, scores, precision=HIGH)
        grad_scores = jnp.einsum("gh,gbk->hbk", mix_pre, grad_mixed, precision=HIGH).astype(
            jnp.bfloat16
        )
        grad_query = (
            jnp.einsum("hbk,khe->bhe", grad_scores, keys_all, preferred_element_type=jnp.float32)
            * scale
        )
        grad_keys = (
            grad_keys
            + jnp.einsum(
                "hbk,bhe->khe", grad_scores, query_block, preferred_element_type=jnp.float32
            )
            * scale
        )
        return ((grad_keys, grad_values, grad_pre, grad_post, grad_shift), grad_query)

    initial = (
        jnp.zeros((count, heads, depth), jnp.float32),
        jnp.zeros((count, heads, depth), jnp.float32),
        jnp.zeros((heads, heads), jnp.float32),
        jnp.zeros((heads, heads), jnp.float32),
        jnp.zeros((heads,), jnp.float32),
    )
    totals, grad_queries = lax.scan(back_block, initial, (queries, masks, log_total, grad_out))
    grad_keys, grad_values, grad_pre, grad_post, grad_shift = totals
    grad_triple = jnp.stack([grad_queries.reshape(count, heads, depth), grad_keys, grad_values], 1)
    grad_triple = grad_triple.reshape(count, 3 * width).astype(jnp.bfloat16)
    grad_entry = contract(normed_low, grad_triple, 0, 0)
    grad_query_bias = jnp.sum(grad_triple[:, :width], 0, dtype=jnp.float32)
    grad_value_bias = jnp.sum(grad_triple[:, 2 * width :], 0, dtype=jnp.float32)
    grad_normed = contract(grad_triple, entry, 1, 1)
    grad_rows, grad_gain, grad_norm_shift = normalize_back(grad_normed, vectors[0], saved)
    talking_grad = jnp.concatenate([grad_pre, grad_post, grad_shift[None]], 0)
    parts = (grad_gain, grad_norm_shift, grad_query_bias, grad_value_bias, grad_bias, grad_scale)
    return (grad + grad_rows, parts, talking_grad, grad_entry, grad_exit)


def class_probs(queries, row_pairs, class_pairs, allowed, scale):
    own = jnp.sum(queries.astype(jnp.float32) * class_pairs[:, 0].astype(jnp.float32), -1) * scale
    others = (
        jnp.einsum("che,rhe->chr", queries, row_pairs[:, 0], preferred_element_type=jnp.float32)
        * scale
    )
    others = jnp.where(allowed[:, None, :], others, NEGATIVE)
    top = jnp.maximum(own, jnp.max(others, -1))
    own_raised = jnp.exp(own - top)
    other_raised = jnp.exp(others - top[..., None])
    total = own_raised + jnp.sum(other_raised, -1)
    return (own_raised / total, other_raised / total[..., None])


def class_forward(rows, classes, vectors, entry, exit_weight, allowed):
    count, width = rows.shape
    slots = classes.shape[0]
    depth = width // HEADS
    scale = depth ** (-0.5)
    normed_rows, saved_rows = normalize(rows, vectors[0], vectors[1])
    normed_class, saved_class = normalize(classes, vectors[0], vectors[1])
    rows_low = normed_rows.astype(jnp.bfloat16)
    class_low = normed_class.astype(jnp.bfloat16)
    pair_bias = jnp.concatenate([jnp.zeros((width,), jnp.float32), vectors[3]])
    queries = (
        jnp.dot(class_low, entry[:, :width], preferred_element_type=jnp.float32) + vectors[2]
    ).astype(jnp.bfloat16)
    row_pairs = (
        jnp.dot(rows_low, entry[:, width:], preferred_element_type=jnp.float32) + pair_bias
    ).astype(jnp.bfloat16)
    class_pairs = (
        jnp.dot(class_low, entry[:, width:], preferred_element_type=jnp.float32) + pair_bias
    ).astype(jnp.bfloat16)
    queries = queries.reshape(slots, HEADS, depth)
    row_pairs = row_pairs.reshape(count, 2, HEADS, depth)
    class_pairs = class_pairs.reshape(slots, 2, HEADS, depth)
    own_exact, other_exact = class_probs(queries, row_pairs, class_pairs, allowed, scale)
    own_low = own_exact.astype(jnp.bfloat16)
    other_low = other_exact.astype(jnp.bfloat16)
    attended = own_low.astype(jnp.float32)[..., None] * class_pairs[:, 1].astype(jnp.float32)
    attended = attended + jnp.einsum(
        "chr,rhe->che", other_low, row_pairs[:, 1], preferred_element_type=jnp.float32
    )
    attended = attended.reshape(slots, width).astype(jnp.bfloat16)
    branch = jnp.dot(attended, exit_weight, preferred_element_type=jnp.float32) + vectors[4]
    cache = (
        saved_rows,
        saved_class,
        rows_low,
        class_low,
        queries,
        row_pairs,
        class_pairs,
        own_exact,
        other_exact,
        own_low,
        other_low,
        attended,
        branch,
    )
    return (classes + vectors[5] * branch, cache)


def class_back(grad, cache, vectors, entry, exit_weight):
    (
        saved_rows,
        saved_class,
        rows_low,
        class_low,
        queries,
        row_pairs,
        class_pairs,
        own_exact,
        other_exact,
        own_low,
        other_low,
        attended,
        branch,
    ) = cache
    count = row_pairs.shape[0]
    slots, width = grad.shape
    depth = width // HEADS
    scale = depth ** (-0.5)
    grad_scale = jnp.sum(grad * branch, 0)
    delta = (vectors[5] * grad).astype(jnp.bfloat16)
    grad_bias = jnp.sum(delta, 0, dtype=jnp.float32)
    grad_exit = contract(attended, delta, 0, 0)
    grad_att = contract(delta, exit_weight, 1, 1).astype(jnp.bfloat16).reshape(slots, HEADS, depth)
    grad_att_wide = grad_att.astype(jnp.float32)
    grad_own_prob = jnp.sum(grad_att_wide * class_pairs[:, 1].astype(jnp.float32), -1)
    grad_other_prob = jnp.einsum(
        "che,rhe->chr", grad_att, row_pairs[:, 1], preferred_element_type=jnp.float32
    )
    grad_class_values = own_low.astype(jnp.float32)[..., None] * grad_att_wide
    grad_row_values = jnp.einsum(
        "chr,che->rhe", other_low, grad_att, preferred_element_type=jnp.float32
    )
    inner = grad_own_prob * own_exact + jnp.sum(grad_other_prob * other_exact, -1)
    grad_own = (own_exact * (grad_own_prob - inner)).astype(jnp.bfloat16)
    grad_other = (other_exact * (grad_other_prob - inner[..., None])).astype(jnp.bfloat16)
    grad_own_wide = grad_own.astype(jnp.float32)[..., None]
    grad_queries = grad_own_wide * class_pairs[:, 0].astype(jnp.float32)
    grad_queries = (
        grad_queries
        + jnp.einsum(
            "chr,rhe->che", grad_other, row_pairs[:, 0], preferred_element_type=jnp.float32
        )
    ) * scale
    grad_class_keys = grad_own_wide * queries.astype(jnp.float32) * scale
    grad_row_keys = (
        jnp.einsum("chr,che->rhe", grad_other, queries, preferred_element_type=jnp.float32) * scale
    )
    grad_queries = grad_queries.reshape(slots, width).astype(jnp.bfloat16)
    grad_row_pairs = (
        jnp.stack([grad_row_keys, grad_row_values], 1)
        .reshape(count, 2 * width)
        .astype(jnp.bfloat16)
    )
    grad_class_pairs = (
        jnp.stack([grad_class_keys, grad_class_values], 1)
        .reshape(slots, 2 * width)
        .astype(jnp.bfloat16)
    )
    grad_entry = jnp.concatenate(
        [
            contract(class_low, grad_queries, 0, 0),
            contract(rows_low, grad_row_pairs, 0, 0) + contract(class_low, grad_class_pairs, 0, 0),
        ],
        1,
    )
    grad_query_bias = jnp.sum(grad_queries, 0, dtype=jnp.float32)
    grad_value_bias = jnp.sum(grad_row_pairs[:, width:], 0, dtype=jnp.float32) + jnp.sum(
        grad_class_pairs[:, width:], 0, dtype=jnp.float32
    )
    grad_normed_rows = contract(grad_row_pairs, entry[:, width:], 1, 1)
    grad_normed_class = contract(grad_queries, entry[:, :width], 1, 1) + contract(
        grad_class_pairs, entry[:, width:], 1, 1
    )
    back_rows, gain_rows, shift_rows = normalize_back(grad_normed_rows, vectors[0], saved_rows)
    back_class, gain_class, shift_class = normalize_back(grad_normed_class, vectors[0], saved_class)
    parts = (
        gain_rows + gain_class,
        shift_rows + shift_class,
        grad_query_bias,
        grad_value_bias,
        grad_bias,
        grad_scale,
    )
    return (back_rows, grad + back_class, parts, grad_entry, grad_exit)


def local(
    patches,
    classes,
    group_size,
    image_count,
    self_entry,
    self_exit,
    self_expand,
    self_reduce,
    self_vectors,
    self_talking,
    self_offset,
    class_entry,
    class_exit,
    class_expand,
    class_reduce,
    class_vectors,
    class_offset,
    patch_cotangent,
    class_cotangent,
):
    count = patches.shape[0]
    slots = classes.shape[0]
    size = group_size[0]
    images = image_count[0]
    place = jnp.arange(count, dtype=jnp.int32)
    segment = place // size
    live = place < images * size
    same = live[:, None] & live[None, :] & (segment[:, None] == segment[None, :])
    allowed_self = same | (place[:, None] == place[None, :])
    slot_ids = jnp.arange(slots, dtype=jnp.int32)
    allowed_class = live[None, :] & (segment[None, :] == slot_ids[:, None])
    columns = (
        lax.all_gather(self_entry, "tensor", axis=1, tiled=True),
        lax.all_gather(self_exit, "tensor", axis=1, tiled=True),
        lax.all_gather(class_entry, "tensor", axis=1, tiled=True),
        lax.all_gather(class_exit, "tensor", axis=1, tiled=True),
    )
    matrices = (
        lax.all_gather(columns[0], "dp", axis=0, tiled=True),
        lax.all_gather(columns[1], "dp", axis=0, tiled=True),
        lax.all_gather(columns[2], "dp", axis=0, tiled=True),
        lax.all_gather(columns[3], "dp", axis=0, tiled=True),
        lax.all_gather(self_expand, "dp", axis=0, tiled=True),
        lax.all_gather(self_reduce, "dp", axis=1, tiled=True),
        lax.all_gather(class_expand, "dp", axis=0, tiled=True),
        lax.all_gather(class_reduce, "dp", axis=1, tiled=True),
    )
    (
        self_in,
        self_out,
        class_in,
        class_out,
        first_expand,
        first_reduce,
        second_expand,
        second_reduce,
    ) = matrices
    share = FF // lax.axis_size("tensor")
    start = lax.axis_index("tensor") * share
    self_part = lax.dynamic_slice_in_dim(self_offset, start, share)
    class_part = lax.dynamic_slice_in_dim(class_offset, start, share)
    rows = patches.astype(jnp.float32)
    middle, self_cache = self_forward(
        rows, self_vectors, self_in, self_out, self_talking, allowed_self
    )
    first, self_feed = feed_forward(middle, self_vectors, first_expand, first_reduce, self_part)
    class_middle, class_cache = class_forward(
        first, classes.astype(jnp.float32), class_vectors, class_in, class_out, allowed_class
    )
    second, class_feed = feed_forward(
        class_middle, class_vectors, second_expand, second_reduce, class_part
    )
    grad_class_middle, class_ff, class_off_grad, class_expand_grad, class_reduce_grad = feed_back(
        class_cotangent.astype(jnp.float32), class_feed, class_vectors, second_expand, second_reduce
    )
    grad_first, grad_classes, class_att, class_entry_grad, class_exit_grad = class_back(
        grad_class_middle, class_cache, class_vectors, class_in, class_out
    )
    grad_first = grad_first + jnp.where(live[:, None], patch_cotangent.astype(jnp.float32), 0.0)
    grad_middle, self_ff, self_off_grad, self_expand_grad, self_reduce_grad = feed_back(
        grad_first, self_feed, self_vectors, first_expand, first_reduce
    )
    grad_rows, self_att, talking_grad, self_entry_grad, self_exit_grad = self_back(
        grad_middle, self_cache, self_vectors, self_in, self_out, self_talking
    )
    self_vector_grad = jnp.stack(self_att + self_ff)
    class_vector_grad = jnp.stack(class_att + class_ff)
    empty = jnp.zeros((FF,), jnp.float32)
    self_off_full = lax.dynamic_update_slice_in_dim(empty, self_off_grad, start, 0)
    class_off_full = lax.dynamic_update_slice_in_dim(empty, class_off_grad, start, 0)
    column_grads = (
        lax.psum_scatter(
            self_entry_grad.astype(jnp.bfloat16), "tensor", scatter_dimension=1, tiled=True
        ).astype(jnp.float32),
        lax.psum_scatter(
            self_exit_grad.astype(jnp.bfloat16), "tensor", scatter_dimension=1, tiled=True
        ).astype(jnp.float32),
        lax.psum_scatter(
            class_entry_grad.astype(jnp.bfloat16), "tensor", scatter_dimension=1, tiled=True
        ).astype(jnp.float32),
        lax.psum_scatter(
            class_exit_grad.astype(jnp.bfloat16), "tensor", scatter_dimension=1, tiled=True
        ).astype(jnp.float32),
    )
    row_grads = (
        lax.psum_scatter(
            column_grads[0].astype(jnp.bfloat16), "dp", scatter_dimension=0, tiled=True
        ).astype(jnp.float32),
        lax.psum_scatter(
            column_grads[1].astype(jnp.bfloat16), "dp", scatter_dimension=0, tiled=True
        ).astype(jnp.float32),
        lax.psum_scatter(
            column_grads[2].astype(jnp.bfloat16), "dp", scatter_dimension=0, tiled=True
        ).astype(jnp.float32),
        lax.psum_scatter(
            column_grads[3].astype(jnp.bfloat16), "dp", scatter_dimension=0, tiled=True
        ).astype(jnp.float32),
        lax.psum_scatter(
            self_expand_grad.astype(jnp.bfloat16), "dp", scatter_dimension=0, tiled=True
        ).astype(jnp.float32),
        lax.psum_scatter(
            self_reduce_grad.astype(jnp.bfloat16), "dp", scatter_dimension=1, tiled=True
        ).astype(jnp.float32),
        lax.psum_scatter(
            class_expand_grad.astype(jnp.bfloat16), "dp", scatter_dimension=0, tiled=True
        ).astype(jnp.float32),
        lax.psum_scatter(
            class_reduce_grad.astype(jnp.bfloat16), "dp", scatter_dimension=1, tiled=True
        ).astype(jnp.float32),
    )
    small = lax.psum(
        (self_vector_grad, talking_grad, self_off_full, class_vector_grad, class_off_full),
        ("dp", "tensor"),
    )
    return (
        first.astype(jnp.bfloat16),
        second.astype(jnp.bfloat16),
        grad_rows,
        grad_classes,
        row_grads[0],
        row_grads[1],
        row_grads[4],
        row_grads[5],
        small[0],
        small[1],
        small[2],
        row_grads[2],
        row_grads[3],
        row_grads[6],
        row_grads[7],
        small[3],
        small[4],
    )


def solution(mesh):
    return jax.shard_map(
        local,
        mesh=mesh,
        in_specs=(
            P(("dp", "tensor"), None),
            P(("dp", "tensor"), None),
            P(("dp", "tensor")),
            P(("dp", "tensor")),
            P("dp", "tensor"),
            P("dp", "tensor"),
            P("dp", "tensor"),
            P("tensor", "dp"),
            P(),
            P(),
            P(),
            P("dp", "tensor"),
            P("dp", "tensor"),
            P("dp", "tensor"),
            P("tensor", "dp"),
            P(),
            P(),
            P(("dp", "tensor"), None),
            P(("dp", "tensor"), None),
        ),
        out_specs=(
            P(("dp", "tensor"), None),
            P(("dp", "tensor"), None),
            P(("dp", "tensor"), None),
            P(("dp", "tensor"), None),
            P("dp", "tensor"),
            P("dp", "tensor"),
            P("dp", "tensor"),
            P("tensor", "dp"),
            P(),
            P(),
            P(),
            P("dp", "tensor"),
            P("dp", "tensor"),
            P("dp", "tensor"),
            P("tensor", "dp"),
            P(),
            P(),
        ),
        check_vma=False,
    )
```

profile of v0, /device:TPU:0, one launch (start us, length us, event | category | flops | bytes accessed | tf_op | source)
XLA Modules:
  0.0 1292.7 jit_solution(4666605391773415840)
XLA Ops:
  25.9 31.6 %all_gather.51 = bf16[384,384]{1,0:T(8,128)(2,1)S(1)} all-gather(bf16[48,384]{1,0:T(8,128)(2,1)S(1)} %bitcast.288), channel_id=1, replica_groups=mesh['dp'=8,'tensor'=4] {'dp'}, dimensions={0}, use_global_device_ids=true | all-gather | bytes 331776 | tf_op jit(solution)/shard_map/all_gather | solution.py:402
  57.5 32.0 %all_gather.49 = bf16[384,1152]{1,0:T(8,128)(2,1)S(1)} all-gather(bf16[48,1152]{1,0:T(8,128)(2,1)S(1)} %bitcast.285), channel_id=1, replica_groups=mesh['dp'=8,'tensor'=4] {'dp'}, dimensions={0}, use_global_device_ids=true | all-gather | bytes 995328 | tf_op jit(solution)/shard_map/all_gather | solution.py:401
  104.3 38.7 %bitcast_reduce_fusion = (f32[8,768]{0,1:T(8,128)S(1)}, f32[768,768,8]{1,2,0:T(8,128)}) fusion(pred[768,768]{1,0:T(8,128)(4,1)S(1)} %fusion.44, f32[17,8]{0,1:T(8,128)S(1)} %copy-done.35, f32[8,768,768]{2,1,0:T(8,128)} %broadcast_multiply_fusion), kind=kOutput, calls=%fused_computation.6 | convolution fusion | flops 462415872 | bytes 38363680 | tf_op jit(solution)/shard_map/while/body/eval_jaxpr/gh,hbk->gbk/dot_general | solution.py:97
  158.6 26.7 %fusion.17 = bf16[8,768,768]{2,0,1:T(8,128)(2,1)} fusion(f32[8]{0:T(128)S(1)} %slice_reduce_fusion, pred[768,768]{1,0:T(8,128)(4,1)S(1)} %fusion.44, f32[768,768,8]{1,2,0:T(8,128)S(1)} %copy-done, f32[8,768]{0,1:T(8,128)} %fusion.15, f32[8,768]{0,1:T(8,128)S(1)} %get-tuple-element.226, f32[17,8]{0,1:T(8,128)S(1)} %copy-done.35), kind=kOutput, calls=%fused_computation.23 | convolution fusion | flops 481296384 | bytes 29913600 | tf_op jit(solution)/shard_map/while/body/eval_jaxpr/gh,hbk->gbk/dot_general | solution.py:102
  196.1 31.0 %all_gather.53 = bf16[384,384]{1,0:T(8,128)(2,1)S(1)} all-gather(bf16[48,384]{1,0:T(8,128)(2,1)S(1)} %copy-done.38), channel_id=1, replica_groups=mesh['dp'=8,'tensor'=4] {'dp'}, dimensions={0}, use_global_device_ids=true | all-gather | bytes 331776 | tf_op jit(solution)/shard_map/all_gather | solution.py:405
  227.1 30.8 %all_gather.54 = bf16[384,384]{0,1:T(8,128)(2,1)S(1)} all-gather(bf16[384,48]{0,1:T(8,128)(2,1)S(1)} %copy-done.39), channel_id=1, replica_groups=mesh['dp'=8,'tensor'=4] {'dp'}, dimensions={1}, use_global_device_ids=true | all-gather | bytes 331776 | tf_op jit(solution)/shard_map/all_gather | solution.py:406
  275.8 32.0 %all_gather.56 = bf16[384,1152]{1,0:T(8,128)(2,1)S(1)} all-gather(bf16[48,1152]{1,0:T(8,128)(2,1)S(1)} %bitcast.284), channel_id=1, replica_groups=mesh['dp'=8,'tensor'=4] {'dp'}, dimensions={0}, use_global_device_ids=true | all-gather | bytes 995328 | tf_op jit(solution)/shard_map/all_gather | solution.py:403
  321.4 31.1 %all_gather.58 = bf16[384,384]{1,0:T(8,128)(2,1)S(1)} all-gather(bf16[48,384]{1,0:T(8,128)(2,1)S(1)} %bitcast.287), channel_id=1, replica_groups=mesh['dp'=8,'tensor'=4] {'dp'}, dimensions={0}, use_global_device_ids=true | all-gather | bytes 331776 | tf_op jit(solution)/shard_map/all_gather | solution.py:404
  352.4 33.1 %all_gather.60 = bf16[384,384]{1,0:T(8,128)(2,1)} all-gather(bf16[48,384]{1,0:T(8,128)(2,1)S(1)} %copy-done.41), channel_id=1, replica_groups=mesh['dp'=8,'tensor'=4] {'dp'}, dimensions={0}, use_global_device_ids=true | all-gather | bytes 331776 | tf_op jit(solution)/shard_map/all_gather | solution.py:407
  385.6 33.0 %all_gather.61 = bf16[384,384]{0,1:T(8,128)(2,1)} all-gather(bf16[384,48]{0,1:T(8,128)(2,1)S(1)} %copy-done.42), channel_id=1, replica_groups=mesh['dp'=8,'tensor'=4] {'dp'}, dimensions={1}, use_global_device_ids=true | all-gather | bytes 331776 | tf_op jit(solution)/shard_map/all_gather | solution.py:408
  478.7 24.6 %reduce-scatter.47.cloned.1.call-done = bf16[288,384]{1,0:T(8,128)(2,1)} async-done(((bf16[1152,384]{1,0:T(8,128)(2,1)}), bf16[288,384]{1,0:T(8,128)(2,1)}) %reduce-scatter.47.cloned.1.call-update) | async-done | bytes 221200
  549.2 28.3 %fusion.18 = bf16[8,768,768]{2,0,1:T(8,128)(2,1)} fusion(f32[8]{0:T(128)S(1)} %copy-done.60, pred[768,768]{1,0:T(8,128)(4,1)S(1)} %fusion.44, f32[768,768,8]{1,2,0:T(8,128)} %get-tuple-element.227, f32[8,768]{0,1:T(8,128)S(1)} %log_add_fusion, f32[17,8]{0,1:T(8,128)S(1)} %copy-done.35), kind=kOutput, calls=%fused_computation.24 | convolution fusion | flops 476577792 | bytes 29889024 | tf_op jit(solution)/shard_map/while/body/eval_jaxpr/gh,hbk->gbk/dot_general | solution.py:102
  592.6 60.0 %reduce-scatter.39.cloned.1.call-done = bf16[48,384]{1,0:T(8,128)(2,1)} async-done(((bf16[384,384]{1,0:T(8,128)(2,1)}), bf16[48,384]{1,0:T(8,128)(2,1)}) %reduce-scatter.39.cloned.1.call-update) | async-done | bytes 36880 | tf_op jit(solution)/shard_map/reduce_scatter | solution.py:486
  654.0 58.8 %reduce-scatter.49.cloned.1.call-done = bf16[48,96]{1,0:T(8,128)(2,1)} async-done(((bf16[384,96]{1,0:T(8,128)(2,1)}), bf16[48,96]{1,0:T(8,128)(2,1)}) %reduce-scatter.49.cloned.1.call-update) | async-done | bytes 9232
  714.4 59.9 %reduce-scatter.35.cloned.1.call-done = bf16[48,288]{1,0:T(8,128)(2,1)} async-done(((bf16[384,288]{1,0:T(8,128)(2,1)}), bf16[48,288]{1,0:T(8,128)(2,1)}) %reduce-scatter.35.cloned.1.call-update) | async-done | bytes 27664 | tf_op jit(solution)/shard_map/reduce_scatter | solution.py:474
  775.9 59.6 %reduce-scatter.33.cloned.1.call-done = bf16[384,48]{0,1:T(8,128)(2,1)} async-done(((bf16[384,384]{0,1:T(8,128)(2,1)}), bf16[384,48]{0,1:T(8,128)(2,1)}) %reduce-scatter.33.cloned.1.call-update) | async-done | bytes 36880 | tf_op jit(solution)/shard_map/reduce_scatter | solution.py:483
  836.9 60.0 %reduce-scatter.31.cloned.1.call-done = bf16[48,384]{1,0:T(8,128)(2,1)} async-done(((bf16[384,384]{1,0:T(8,128)(2,1)}), bf16[48,384]{1,0:T(8,128)(2,1)}) %reduce-scatter.31.cloned.1.call-update) | async-done | bytes 36880 | tf_op jit(solution)/shard_map/reduce_scatter | solution.py:480
  898.3 33.2 %reduce-scatter.25.cloned.1.call-done = bf16[768,384]{1,0:T(8,128)(2,1)} async-done(((bf16[3072,384]{1,0:T(8,128)(2,1)}), bf16[768,384]{1,0:T(8,128)(2,1)}) %reduce-scatter.25.cloned.1.call-update) | async-done | bytes 589840 | tf_op jit(solution)/shard_map/reduce_scatter | solution.py:76
  947.8 42.6 %fusion = (f32[8,768]{0,1:T(8,128)S(1)}, f32[768,768,8]{1,2,0:T(8,128)}) fusion(f32[8,768]{0,1:T(8,128)S(1)} %log_add_fusion, f32[768,768,8]{1,2,0:T(8,128)} %get-tuple-element.227, pred[768,768]{1,0:T(8,128)(4,1)S(1)} %fusion.44, f32[17,8]{0,1:T(8,128)S(1)} %copy-done.35, f32[8,768,768]{2,1,0:T(8,128)} %get-tuple-element.242), kind=kOutput, calls=%fused_computation.2 | convolution fusion | flops 471853056 | bytes 57262624 | tf_op jit(solution)/shard_map/while/body/eval_jaxpr/gh,gbk->hbk/dot_general | solution.py:171
  990.4 28.8 %convert_bitcast_fusion = bf16[8,768,768]{2,0,1:T(8,128)(2,1)} fusion(f32[768,768,8]{1,2,0:T(8,128)} %get-tuple-element.238, f32[8,768]{0,1:T(8,128)S(1)} %get-tuple-element.237, f32[8,768]{0,1:T(8,128)S(1)} %log_add_fusion, f32[768,768,8]{1,2,0:T(8,128)} %get-tuple-element.227, pred[768,768]{1,0:T(8,128)(4,1)S(1)} %fusion.44, f32[17,8]{0,1:T(8,128)S(1)} %copy-done.35), kind=kOutput, calls=%fused_computation.29 | convolution fusion | flops 476577792 | bytes 47825440 | tf_op jit(solution)/shard_map/while/body/eval_jaxpr/gh,gbk->hbk/dot_general | solution.py:174
  1055.4 50.0 %fusion.108 = f32[8,8]{0,1:T(8,128)S(1)} fusion(f32[8,768,768]{2,1,0:T(8,128)} %broadcast_multiply_fusion, f32[8,768,768]{2,0,1:T(8,128)} %fusion.254), kind=kOutput, calls=%fused_computation.157 | convolution fusion | flops 452984832 | bytes 37748992 | tf_op jit(solution)/shard_map/while/body/eval_jaxpr/gbk,hbk->gh/dot_general | solution.py:173
  1113.9 50.2 %fusion.113 = f32[8,8]{0,1:T(8,128)S(1)} fusion(f32[768,768,8]{1,2,0:T(8,128)} %get-tuple-element.227, f32[8,768]{0,1:T(8,128)S(1)} %log_add_fusion, pred[768,768]{1,0:T(8,128)(4,1)S(1)} %fusion.44, f32[8,768,768]{2,1,0:T(8,128)} %get-tuple-element.242), kind=kOutput, calls=%fused_computation.158 | convolution fusion | flops 462422016 | bytes 38363392 | tf_op jit(solution)/shard_map/while/body/eval_jaxpr/gbk,hbk->gh/dot_general | solution.py:170
  1167.9 41.0 %all-reduce.3 = (f32[10,384]{1,0:T(8,128)}, f32[17,8]{0,1:T(8,128)}, f32[1536]{0:T(1024)}, f32[10,384]{1,0:T(8,128)}, f32[1536]{0:T(1024)}) all-reduce(f32[10,384]{1,0:T(8,128)S(1)} %stack.107, f32[17,8]{0,1:T(8,128)S(1)} %pad_maximum_fusion.5, ...), channel_id=1, replica_groups=mesh['dp'=8,'tensor'=4] {'dp','tensor'}, use_global_device_ids=true, to_apply=%region_48.49 | all-reduce | flops 10888 | bytes 87104 | tf_op jit(solution)/shard_map/psum | solution.py:493
  1225.2 59.1 %reduce-scatter.43.cloned.1.call-done = bf16[48,288]{1,0:T(8,128)(2,1)} async-done(((bf16[384,288]{1,0:T(8,128)(2,1)}), bf16[48,288]{1,0:T(8,128)(2,1)}) %reduce-scatter.43.cloned.1.call-update) | async-done | bytes 27664
  (360 shorter events, 299.3 us)
Async XLA Ops:
  7.2 250.7 %all-gather.9.cloned.1.call-start = ((), (), s32[]{:S(2)}) async-start(), calls=%async_computation.14 | async-start | bytes 2949120 | tf_op jit(solution)/shard_map/all_gather | solution.py:53
  9.4 149.2 %copy-start.59 = (f32[8]{0:T(128)}, f32[8]{0:T(128)S(1)}, u32[]{:S(2)}) copy-start(f32[8]{0:T(128)S(1)} %slice_reduce_fusion) | copy-start | bytes 100
  10.8 82.2 %copy-start.36 = (f32[768]{0:T(1024)}, f32[768]{0:T(1024)S(1)}, u32[]{:S(2)}) copy-start(f32[768]{0:T(1024)S(1)} %broadcast_multiply_fusion.9) | copy-start | bytes 9220
  57.5 134.6 %copy-start.15 = (bf16[384,384]{1,0:T(8,128)(2,1)}, bf16[384,384]{1,0:T(8,128)(2,1)S(1)}, u32[]{:S(2)}) copy-start(bf16[384,384]{1,0:T(8,128)(2,1)S(1)} %all_gather.51) | copy-start | bytes 884740
  195.3 223.3 %reduce-scatter.23.cloned.1.call-start = ((), (), s32[]{:S(2)}) async-start(), calls=%async_computation.15 | async-start | bytes 2949120 | tf_op jit(solution)/shard_map/reduce_scatter | solution.py:56
  268.5 84.0 %copy-start.41 = (bf16[48,384]{1,0:T(8,128)(2,1)S(1)}, bf16[48,384]{1,0:T(8,128)(2,1)}, u32[]{:S(2)}) copy-start(bf16[48,384]{1,0:T(8,128)(2,1)} %param.32) | copy-start | bytes 110596
  268.5 208.6 %reduce-scatter.37.cloned.1.call-start = ((), (), s32[]{:S(2)}) async-start(), calls=%async_computation.23 | async-start | bytes 368640 | tf_op jit(solution)/shard_map/reduce_scatter | solution.py:463
  274.6 110.9 %copy-start.42 = (bf16[384,48]{0,1:T(8,128)(2,1)S(1)}, bf16[384,48]{0,1:T(8,128)(2,1)}, u32[]{:S(2)}) copy-start(bf16[384,48]{0,1:T(8,128)(2,1)} %param.33) | copy-start | bytes 110596
  275.0 145.0 %copy-start.51 = (f32[3]{0:T(128)}, f32[3]{0:T(128)S(1)}, u32[]{:S(2)}) copy-start(f32[3]{0:T(128)S(1)} %broadcast_multiply_fusion.15) | copy-start | bytes 40
  275.8 144.2 %copy-start.53 = (f32[3]{0:T(128)}, f32[3]{0:T(128)S(1)}, u32[]{:S(2)}) copy-start(f32[3]{0:T(128)S(1)} %add_rsqrt_fusion.4) | copy-start | bytes 40
  307.8 110.8 %copy-start.21 = (bf16[384,1152]{1,0:T(8,128)(2,1)}, bf16[384,1152]{1,0:T(8,128)(2,1)S(1)}, u32[]{:S(2)}) copy-start(bf16[384,1152]{1,0:T(8,128)(2,1)S(1)} %all_gather.56) | copy-start | bytes 2654212
  456.2 47.2 %reduce-scatter.47.cloned.1.call-start = ((), (), s32[]{:S(2)}) async-start(), calls=%async_computation.28 | async-start | bytes 1105920
  466.1 62.9 %all-gather.11.cloned.1.call-start = ((), (), s32[]{:S(2)}) async-start(), calls=%async_computation.16 | async-start | bytes 2949120 | tf_op jit(solution)/shard_map/all_gather | solution.py:71
  472.7 118.4 %reduce-scatter.41.cloned.1.call-start = ((), (), s32[]{:S(2)}) async-start(), calls=%async_computation.25 | async-start | bytes 331776 | tf_op jit(solution)/shard_map/reduce_scatter | solution.py:489
  473.8 178.8 %reduce-scatter.39.cloned.1.call-start = ((), (), s32[]{:S(2)}) async-start(), calls=%async_computation.24 | async-start | bytes 331776 | tf_op jit(solution)/shard_map/reduce_scatter | solution.py:486
  474.9 238.0 %reduce-scatter.49.cloned.1.call-start = ((), (), s32[]{:S(2)}) async-start(), calls=%async_computation.29 | async-start | bytes 110592
  478.7 295.6 %reduce-scatter.35.cloned.1.call-start = ((), (), s32[]{:S(2)}) async-start(), calls=%async_computation.22 | async-start | bytes 331776 | tf_op jit(solution)/shard_map/reduce_scatter | solution.py:474
  505.2 330.3 %reduce-scatter.33.cloned.1.call-start = ((), (), s32[]{:S(2)}) async-start(), calls=%async_computation.21 | async-start | bytes 331776 | tf_op jit(solution)/shard_map/reduce_scatter | solution.py:483
  533.5 363.4 %reduce-scatter.31.cloned.1.call-start = ((), (), s32[]{:S(2)}) async-start(), calls=%async_computation.20 | async-start | bytes 331776 | tf_op jit(solution)/shard_map/reduce_scatter | solution.py:480
  543.2 388.2 %reduce-scatter.25.cloned.1.call-start = ((), (), s32[]{:S(2)}) async-start(), calls=%async_computation.17 | async-start | bytes 2949120 | tf_op jit(solution)/shard_map/reduce_scatter | solution.py:76
  548.0 616.1 %reduce-scatter.29.cloned.1.call-start = ((), (), s32[]{:S(2)}) async-start(), calls=%async_computation.19 | async-start | bytes 368640 | tf_op jit(solution)/shard_map/reduce_scatter | solution.py:457
  1048.8 117.2 %reduce-scatter.27.cloned.1.call-start = ((), (), s32[]{:S(2)}) async-start(), calls=%async_computation.18 | async-start | bytes 1105920 | tf_op jit(solution)/shard_map/reduce_scatter | solution.py:454
  1113.8 109.9 %reduce-scatter.45.cloned.1.call-start = ((), (), s32[]{:S(2)}) async-start(), calls=%async_computation.27 | async-start | bytes 110592
  1165.9 118.4 %reduce-scatter.43.cloned.1.call-start = ((), (), s32[]{:S(2)}) async-start(), calls=%async_computation.26 | async-start | bytes 331776
  (56 other events, 843.6 us)
Sparse Core Ops, SparseCore 0:
  195.4 25.4 all-gather.8
  268.6 34.1 reduce-scatter.22
  456.3 20.6 reduce-scatter.36
  479.5 23.8 reduce-scatter.46
  504.8 24.0 all-gather.10
  532.4 58.7 reduce-scatter.40
  594.8 57.7 reduce-scatter.38
  656.2 56.6 reduce-scatter.48
  716.5 57.7 reduce-scatter.34
  777.8 57.6 reduce-scatter.32
  839.1 57.6 reduce-scatter.30
  899.4 31.9 reduce-scatter.24
  1048.9 20.2 reduce-scatter.28
  1113.9 23.9 reduce-scatter.26
  1166.0 57.6 reduce-scatter.44
  1226.9 57.3 reduce-scatter.42
where the time goes:
time: 1300 us; the launch traced here: 1290 us
  waiting for transfers between devices  464 us (36%)
  matrix products  365 us (28%)
  blocking collectives  341 us (26%)
  other arithmetic  69.7 us (5%)
  local copies, waits for them, and re-layouts  35.1 us (3%)
  between operations  17.2 us (1%)
    unnamed x20, waiting for transfers between devices  155 us
    reduce_scatter x1, waiting for transfers between devices, local(): lax.psum_scatter(class_expand_grad.astype(jnp.bfloat16), 'dp', scatter_di...  60 us
    reduce_scatter x1, waiting for transfers between devices, local(): lax.psum_scatter(self_expand_grad.astype(jnp.bfloat16), 'dp', scatter_dim...  60 us
    reduce_scatter x1, waiting for transfers between devices, local(): lax.psum_scatter(column_grads[2].astype(jnp.bfloat16), 'dp', scatter_dime...  59.9 us
    reduce_scatter x1, waiting for transfers between devices, local(): lax.psum_scatter(self_reduce_grad.astype(jnp.bfloat16), 'dp', scatter_dim...  59.6 us
    dot_general x2, matrix products, post_weights(): jnp.einsum('gh,hbk->gbk', mix_post, probs, precision=HIGH)  55 us
    dot_general x1, matrix products, back_block(): jnp.einsum('gbk,hbk->gh', grad_weights, probs, precision=HIGH)  50.2 us
    dot_general x1, matrix products, back_block(): jnp.einsum('gbk,hbk->gh', grad_mixed, scores, precision=HIGH)  50 us
  transfers between devices with their start and end apart: 16, of which 12 were waited for; matrix products, arithmetic and copies ran while one was open for 16% of the time, Pallas kernels for 0%

commit v1 on v0

v1 whole, which is shorter than its diff:
```python
import functools

import jax
import jax.numpy as jnp
from jax import lax
from jax.experimental import pallas as pl
from jax.experimental.pallas import tpu as pltpu
from jax.sharding import PartitionSpec as P

HEADS = 8
EPSILON = 1e-06
NEGATIVE = -1e30
ROOT_HALF = 0.7071067811865476
ROOT_TWO_PI = 2.5066282746310002
WIDE = jnp.float32
LOW = jnp.bfloat16

WIDTH = 384
DEPTH = WIDTH // HEADS
ROWS = 768
FF = 1536
PARTS = 4
COLS = 3 * WIDTH // PARTS
TILE = 128
SPAN = HEADS * TILE
HALVES = (slice(0, SPAN // 2), slice(SPAN // 2, SPAN))
WIDE_HALVES = (slice(0, FF // 2), slice(FF // 2, FF))
SHARD = 48
DEPS = 4
STEPS = ROWS // TILE
TOGETHER = 1
KEYS = ROWS + 128
DENSE = 384
PAIRS = HEADS * 8


def nn(a, b):
    return lax.dot_general(a, b, (((1,), (0,)), ((), ())), preferred_element_type=WIDE)


def nt(a, b):
    return lax.dot_general(a, b, (((1,), (1,)), ((), ())), preferred_element_type=WIDE)


def iota(shape, dim):
    return lax.broadcasted_iota(jnp.int32, shape, dim)


def rows_at(i, size):
    return pl.ds(pl.multiple_of(i * size, size), size)


def normalize(x, gain, shift):
    mean = jnp.mean(x, -1, keepdims=True)
    centered = x - mean
    inverse = lax.rsqrt(jnp.mean(centered * centered, -1, keepdims=True) + EPSILON)
    unit = centered * inverse
    return unit * gain + shift, unit, inverse


def keep_stats(r, k, rows, x, inverse):
    r.stats[rows, 2 * k : 2 * k + 1] = jnp.mean(x, -1, keepdims=True)
    r.stats[rows, 2 * k + 1 : 2 * k + 2] = inverse


def unit_of(r, k, rows, x):
    inverse = r.stats[rows, 2 * k + 1 : 2 * k + 2]
    return (x - r.stats[rows, 2 * k : 2 * k + 1]) * inverse, inverse


def normalize_back(grad, gain, unit, inverse):
    scaled = grad * gain
    inner = jnp.mean(scaled * unit, -1, keepdims=True)
    return inverse * (scaled - jnp.mean(scaled, -1, keepdims=True) - unit * inner)


def by_head(x):
    return jnp.sum(x.reshape(HEADS, DEPTH, x.shape[-1]), 1)


def total(x):
    return jnp.sum(x, 0, keepdims=True)


def smooth(hidden):
    cdf = 0.5 * (1.0 + lax.erf(hidden * ROOT_HALF))
    slope = cdf + hidden * jnp.exp(-0.5 * hidden * hidden) * (1.0 / ROOT_TWO_PI)
    return (hidden * cdf).astype(LOW), slope.astype(LOW)


def each(count, together, step, points):
    def some(i, c):
        for k in range(together):

            def at(where):
                for key, todo in points.items():
                    t, place = divmod(key, 2)
                    if place == where and t % together == k:
                        pl.when(i == t // together)(todo)

            step(i * together + k, at)
        return c

    lax.fori_loop(0, count // together, some, 0)


class Refs:
    def __init__(self, **refs):
        self.__dict__.update(refs)


SCRATCH = dict(
    cols=((WIDTH, 128), WIDE),
    pad=((128, 128), WIDE),
    patches=((ROWS, WIDTH), LOW),
    cot=((ROWS, WIDTH), LOW),
    result=((ROWS, WIDTH), LOW),
    grad=((ROWS, WIDTH), WIDE),
    n1=((ROWS, WIDTH), LOW),
    stats=((ROWS, 128), WIDE),
    went=((3 * WIDTH, WIDTH), LOW),
    wout=((WIDTH, WIDTH), LOW),
    wback=((WIDTH, WIDTH), LOW),
    wfull=((WIDTH, 3 * WIDTH), LOW),
    qt=((WIDTH, ROWS), LOW),
    kext=((ROWS, 512), LOW),
    kt=((WIDTH, ROWS), LOW),
    vext=((ROWS, 512), LOW),
    vt=((WIDTH, ROWS), LOW),
    hot=((ROWS, 128), LOW),
    hott=((8, ROWS), WIDE),
    vsum=((WIDTH, 128), WIDE),
    gsum=((WIDTH, 128), WIDE),
    qm=((512, SPAN), LOW),
    qn=((WIDTH, SPAN), LOW),
    gm=((ROWS, SPAN), LOW),
    et=((STEPS, ROWS, SPAN), LOW),
    un=((STEPS, WIDTH, SPAN), LOW),
    linv=((STEPS, 1, SPAN), WIDE),
    attt=((WIDTH, ROWS), LOW),
    middle=((ROWS, WIDTH), WIDE),
    branch1=((ROWS, WIDTH), LOW),
    branch2=((ROWS, WIDTH), WIDE),
    n2t=((WIDTH, ROWS), LOW),
    act=((ROWS, FF), LOW),
    slope=((ROWS, FF), LOW),
    next=((KEYS, WIDTH), LOW),
    wout_c=((WIDTH, WIDTH), LOW),
    small8=((8, WIDTH), WIDE),
    cot8=((8, WIDTH), WIDE),
    both=((KEYS, 128), LOW),
    qkwv=((128, WIDTH), LOW),
    d1t=((WIDTH, ROWS), LOW),
    d2t=((WIDTH, ROWS), LOW),
    dot=((WIDTH, ROWS), LOW),
    gwout=((WIDTH, WIDTH), WIDE),
    offset=((1, FF), WIDE),
    dvt=((WIDTH, ROWS), WIDE),
    dkt=((WIDTH, ROWS), WIDE),
    accp=((HEADS, HEADS, TILE), WIDE),
    accq=((HEADS, HEADS, TILE), WIDE),
    dtr=((3 * WIDTH, ROWS), LOW),
)


def block_of(w, j):
    return w[j].reshape(WIDTH, w.shape[-1])


def whole_of(w):
    return w[...].reshape(WIDTH, FF)


def as_block(x):
    return x.reshape(DEPS, 2, SHARD, x.shape[-1])


def unpack_weights(wa, went, wout):
    for j in range(PARTS):
        block = block_of(wa, j).T
        went[COLS * j : COLS * (j + 1), :] = block[:COLS]
        wout[96 * j : 96 * (j + 1), :] = block[COLS:]

def columns(r):
    r.pad[...] = jnp.zeros((128, 128), WIDE)
    r.pad[0:8, 0:17] = r.talking[...]
    turned = r.pad[...]
    talk = turned.T
    turned = turned[0:8]
    moved = pltpu.roll(talk, 8, 1)[8:16]
    lane = iota((8, 128), 1)
    alone = jnp.sum(talk[8:16], 1, keepdims=True) + turned[:, 16:17]
    base = jnp.where(lane < 8, turned * DEPTH ** (-0.5), moved)
    base = jnp.where(lane == 16, turned, base)
    base = jnp.where(lane == 19, alone, base)
    turned = r.vec[0:8, :].T
    lane = iota((DEPTH, 128), 1)
    for h in range(HEADS):
        rows = slice(DEPTH * h, DEPTH * (h + 1))
        x = jnp.broadcast_to(base[h : h + 1], (DEPTH, 128))
        x = jnp.where(lane == 17, turned[rows, 2:3], x)
        r.cols[rows, :] = jnp.where(lane == 18, turned[rows, 3:4], x)


def masks(r):
    size, images = r.size[0], r.images[0]
    place = iota((ROWS, 128), 0)
    which = iota((ROWS, 128), 1)
    inside = (place >= which * size) & (place < which * size + size) & (which < images)
    r.hot[...] = jnp.where(inside, 1.0, 0.0).astype(LOW)
    r.kext[:, WIDTH:] = jnp.where(inside | (which >= 3), 0.0, NEGATIVE).astype(LOW)
    r.vext[:, WIDTH:] = jnp.where(which < 2, 1.0, 0.0).astype(LOW)
    place = iota((8, ROWS), 1)
    which = iota((8, ROWS), 0)
    inside = (place >= which * size) & (place < which * size + size) & (which < images)
    r.hott[...] = jnp.where(inside, 1.0, 0.0)


def norm_first(r):
    gain, shift = r.vec[0:1, :], r.vec[1:2, :]

    def norm_step(i, c):
        rows = rows_at(i, DENSE)
        x = r.patches[rows, :].astype(WIDE)
        normed, unit, inverse = normalize(x, gain, shift)
        r.n1[rows, :] = normed.astype(LOW)
        keep_stats(r, 0, rows, x, inverse)
        return c

    lax.fori_loop(0, ROWS // DENSE, norm_step, 0)


def project(r):
    unpack_weights(r.wa, r.went, r.wout)

    def step(i, c):
        rows = rows_at(i, DENSE)
        normed = r.n1[rows, :]
        turned = nt(r.went[...], normed)
        r.qt[:, rows] = (turned[0:WIDTH] + r.cols[:, 17:18]).astype(LOW)
        r.kt[:, rows] = turned[WIDTH : 2 * WIDTH].astype(LOW)
        r.vt[:, rows] = (turned[2 * WIDTH :] + r.cols[:, 18:19]).astype(LOW)
        both = nt(normed, r.went[WIDTH:, :])
        r.kext[rows, 0:WIDTH] = both[:, 0:WIDTH].astype(LOW)
        r.vext[rows, 0:WIDTH] = (both[:, WIDTH:] + r.vec[3:4, :]).astype(LOW)
        return c

    lax.fori_loop(0, ROWS // DENSE, step, 0)
    r.vsum[...] = nn(r.vt[...], r.hot[...])
    r.wback[...] = r.wout[...].T
    r.wfull[...] = r.went[...].T


def attend(r, points):
    def step(t, at):
        at(0)
        rows = rows_at(t, TILE)
        q = r.qt[:, rows].astype(WIDE)
        hot = r.hott[:, rows]
        hot_rows = jnp.concatenate([hot, jnp.zeros((120, TILE), WIDE)], 0).astype(LOW)
        for g in range(HEADS):
            r.qm[0:WIDTH, TILE * g : TILE * (g + 1)] = (q * r.cols[:, g : g + 1]).astype(LOW)
            r.qm[WIDTH:, TILE * g : TILE * (g + 1)] = hot_rows
        own = r.vt[:, rows].astype(WIDE)
        att = r.cols[:, 16:17] * (
            r.vsum[:, 0:1] * hot[0:1] + r.vsum[:, 1:2] * hot[1:2] + r.vsum[:, 2:3] * hot[2:3]
        )
        for half in HALVES:
            scores = nn(r.kext[...], r.qm[:, half])
            raised = jnp.exp(scores - jnp.max(scores, 0, keepdims=True))
            r.linv[t, :, half] = 1.0 / jnp.sum(raised, 0, keepdims=True)
            r.et[t, :, half] = raised.astype(LOW)
        at(1)
        for i, half in enumerate(HALVES):
            mean = nn(r.vt[...], r.et[t, :, half]) * r.linv[t, :, half]
            r.un[t, :, half] = mean.astype(LOW)
            for k in range(HEADS // 2):
                h = HEADS // 2 * i + k
                att = att + r.cols[:, 8 + h : 9 + h] * mean[:, TILE * k : TILE * (k + 1)]
        live = (hot[0:1] + hot[1:2] + hot[2:3]) > 0.5
        att = jnp.where(live, att, r.cols[:, 19:20] * own).astype(LOW)
        r.attt[:, rows] = att
        branch = nt(att.T, r.wout[...]) + r.vec[4:5, :]
        r.branch1[rows, :] = branch.astype(LOW)
        r.middle[rows, :] = r.patches[rows, :].astype(WIDE) + r.vec[5:6, :] * branch

    each(STEPS, TOGETHER, step, points)


def feed(r, points):
    def step(i, at):
        at(0)
        rows = rows_at(i, DENSE)
        middle = r.middle[rows, :]
        normed, unit, inverse = normalize(middle, r.vec[6:7, :], r.vec[7:8, :])
        keep_stats(r, 1, rows, middle, inverse)
        normed = normed.astype(LOW)
        r.n2t[:, rows] = normed.T
        hidden = [nn(normed, whole_of(r.we)[:, half]) + r.off[half].reshape(1, FF // 2) for half in WIDE_HALVES]
        for half, part in zip(WIDE_HALVES, hidden, strict=True):
            active, slope = smooth(part)
            r.act[rows, half] = active
            r.slope[rows, half] = slope
        at(1)
        lifted = nt(whole_of(r.wr), r.act[rows, :]).T
        branch = lifted + r.vec[8:9, :]
        r.branch2[rows, :] = branch
        first = middle + r.vec[9:10, :] * branch
        r.result[rows, :] = first.astype(LOW)
        normed, unit, inverse = normalize(first, r.vec_c[0:1, :], r.vec_c[1:2, :])
        r.next[rows, :] = normed.astype(LOW)
        keep_stats(r, 2, rows, first, inverse)

    each(ROWS // DENSE, 1, step, points)


def classes(r):
    v = lambda k: r.vec_c[k : k + 1, :]
    scale = DEPTH ** (-0.5)
    unpack_weights(r.wa_c, r.went, r.wout_c)
    wq, wk, wv = (r.went[WIDTH * k : WIDTH * (k + 1), :] for k in range(3))
    r.small8[...] = jnp.zeros((8, WIDTH), WIDE)
    r.cot8[...] = jnp.zeros((8, WIDTH), WIDE)
    r.small8[0:3, :] = r.classes[...].astype(WIDE)
    r.cot8[0:3, :] = r.class_cot[...].astype(WIDE)
    tokens = r.small8[...]
    normed, unit, inverse = normalize(tokens, v(0), v(1))
    low = normed.astype(LOW)
    valid = iota((128, WIDTH), 0) < 3
    r.next[ROWS:, :] = jnp.where(
        valid, jnp.concatenate([normed, jnp.zeros((120, WIDTH), WIDE)], 0), 0.0
    ).astype(LOW)
    head_of = iota((PAIRS, WIDTH), 1) // DEPTH
    own_head = head_of == iota((PAIRS, WIDTH), 0) // 8

    def spread(x):
        return jnp.where(own_head, jnp.concatenate([x] * HEADS, 0), 0.0)

    def gather_heads(x):
        x = jnp.where(own_head, x, 0.0)
        out = x[0:8]
        for h in range(1, HEADS):
            out = out + x[8 * h : 8 * (h + 1)]
        return out

    queries = (nt(low, wq) + v(2)).astype(LOW)
    qexp = spread(queries.astype(WIDE))
    qk = (nn(qexp.astype(LOW), wk) * scale).astype(LOW)
    keys = r.next[...]
    scores = nt(qk, keys)
    size, images = r.size[0], r.images[0]
    slot = iota((PAIRS, KEYS), 0) & 7
    place = iota((PAIRS, KEYS), 1)
    allowed = (place >= slot * size) & (place < slot * size + size) & (slot < images)
    allowed = allowed | (place == slot + ROWS)
    scores = jnp.where(allowed, scores, NEGATIVE)
    raised = jnp.exp(scores - jnp.max(scores, -1, keepdims=True))
    probs = raised / jnp.sum(raised, -1, keepdims=True)
    probs_low = probs.astype(LOW)
    mass = jnp.sum(probs_low.astype(WIDE), -1, keepdims=True)
    z = nn(probs_low, keys).astype(LOW)
    attended = gather_heads(nt(z, wv) + mass * v(3)).astype(LOW)
    branch = nt(attended, r.wout_c[...]) + v(4)
    middle = tokens + v(5) * branch
    normed2, unit2, inverse2 = normalize(middle, v(6), v(7))
    low2 = normed2.astype(LOW)
    expand, reduce = whole_of(r.we_c), whole_of(r.wr_c)
    hidden = nn(low2, expand) + r.off_c[...].reshape(1, FF)
    active, slope = smooth(hidden)
    lifted = nt(active, reduce)
    branch2 = lifted + v(8)
    second = middle + v(9) * branch2
    r.class_result[...] = second[0:3].astype(LOW)
    grad = r.cot8[...]
    grad_scale2 = total(grad * branch2)
    delta2 = (v(9) * grad).astype(LOW)
    grad_bias2 = total(delta2.astype(WIDE))
    low2_t, delta2_t = low2.astype(WIDE).T.astype(LOW), delta2.astype(WIDE).T.astype(LOW)
    grad_hidden = (nn(delta2, reduce) * slope.astype(WIDE)).astype(LOW)
    off = total(grad_hidden.astype(WIDE))
    for j in range(PARTS):
        r.early[0, 20 + j : 21 + j, :] = off[:, WIDTH * j : WIDTH * (j + 1)]
    back = nt(grad_hidden, expand)
    r.we_c[...] = as_block(nn(low2_t, grad_hidden).astype(LOW))
    r.wr_c[...] = as_block(nn(delta2_t, active).astype(LOW))
    grad_gain2, grad_shift2 = total(back * unit2), total(back)
    grad = grad + normalize_back(back, v(6), unit2, inverse2)
    grad_scale = total(grad * branch)
    delta = (v(5) * grad).astype(LOW)
    grad_bias = total(delta.astype(WIDE))
    gatt = nn(delta, r.wout_c[...]).astype(LOW)
    dexp = spread(gatt.astype(WIDE))
    wide_v = nn(dexp.astype(LOW), wv).astype(LOW)
    gp = nt(wide_v, keys)
    ds = (probs * (gp - jnp.sum(gp * probs, -1, keepdims=True))).astype(LOW)
    y = nn(ds, keys).astype(LOW)
    gq = (gather_heads(nt(y, wk)) * scale).astype(LOW)
    both = jnp.concatenate([ds.astype(WIDE), probs_low.astype(WIDE)], 0).T.astype(LOW)
    r.both[...] = both
    r.qkwv[...] = jnp.concatenate([qk, wide_v], 0)
    grad_normed = nn(both[ROWS:, :], r.qkwv[...])[0:8] + nn(gq, wq)
    r.class_grad[...] = (grad + normalize_back(grad_normed, v(0), unit, inverse))[0:3]
    valid8 = iota((8, WIDTH), 0) < 3
    grad_normed = jnp.where(valid8, grad_normed, 0.0)
    gq_t = gq.astype(WIDE).T.astype(LOW)
    grad_q = nn(gq_t, low)
    grad_k = nn((qexp * scale).T.astype(LOW), y)
    grad_v = nn(dexp.T.astype(LOW), z)
    grad_out = nn(delta.astype(WIDE).T.astype(LOW), attended)
    whole = jnp.concatenate([grad_q, grad_k, grad_v], 0)
    for j in range(PARTS):
        block = jnp.concatenate(
            [whole[COLS * j : COLS * (j + 1)], grad_out[96 * j : 96 * (j + 1)]], 0
        )
        r.wa_c[j] = as_block(block.T.astype(LOW))
    grad_vb = total(jnp.where(own_head, mass * dexp, 0.0))
    r.early[0, 10:20, :] = jnp.concatenate(
        [
            total(grad_normed * unit),
            total(grad_normed),
            total(gq.astype(WIDE)),
            grad_vb,
            grad_bias,
            grad_scale,
            grad_gain2,
            grad_shift2,
            grad_bias2,
            grad_scale2,
        ],
        0,
    )


def feed_back(r, points):
    size, images = r.size[0], r.images[0]
    r.early[0, 0:10, :] = jnp.zeros((10, WIDTH), WIDE)
    r.offset[...] = jnp.zeros((1, FF), WIDE)

    def add(k, x):
        r.early[0, k - 4 : k - 3, :] += total(x)

    def step(i, at):
        at(0)
        rows = rows_at(i, DENSE)
        branch2 = r.branch2[rows, :]
        unitc, inversec = unit_of(r, 2, rows, r.middle[rows, :] + r.vec[9:10, :] * branch2)
        dn = nn(r.both[rows, :], r.qkwv[...])
        add(14, dn * unitc)
        add(15, dn)
        grad = normalize_back(dn, r.vec_c[0:1, :], unitc, inversec)
        place = iota((DENSE, WIDTH), 0) + i * DENSE
        grad = grad + jnp.where(place < size * images, r.cot[rows, :].astype(WIDE), 0.0)
        add(9, grad * branch2)
        delta = (r.vec[9:10, :] * grad).astype(LOW)
        add(8, delta.astype(WIDE))
        r.d2t[:, rows] = delta.T
        grad_hidden = [
            (nn(delta, whole_of(r.wr)[:, half]) * r.slope[rows, half].astype(WIDE)).astype(LOW)
            for half in WIDE_HALVES
        ]
        for half, part in zip(WIDE_HALVES, grad_hidden, strict=True):
            r.slope[rows, half] = part
            r.offset[:, half] += total(part.astype(WIDE))
        at(1)
        back = nt(whole_of(r.we), r.slope[rows, :]).T
        unit, inverse = unit_of(r, 1, rows, r.middle[rows, :])
        add(6, back * unit)
        add(7, back)
        grad = grad + normalize_back(back, r.vec[6:7, :], unit, inverse)
        r.grad[rows, :] = grad
        add(5, grad * r.branch1[rows, :].astype(WIDE))
        delta = (r.vec[5:6, :] * grad).astype(LOW)
        add(4, delta.astype(WIDE))
        r.d1t[:, rows] = delta.T
        r.dot[:, rows] = nt(r.wback[...], delta).astype(LOW)

    each(ROWS // DENSE, 1, step, points)
    for half in WIDE_HALVES:
        r.we[:, :, :, half] = as_block(nn(r.n2t[...], r.slope[:, half]).astype(LOW))
        r.wr[:, :, :, half] = as_block(nn(r.d2t[...], r.act[:, half]).astype(LOW))
    for j in range(PARTS):
        r.early[0, 6 + j : 7 + j, :] = r.offset[:, WIDTH * j : WIDTH * (j + 1)]
    r.gwout[...] = nt(r.d1t[...], r.attt[...])


def attend_back(r, points):
    r.dvt[...] = jnp.zeros((WIDTH, ROWS), WIDE)
    r.dkt[...] = jnp.zeros((WIDTH, ROWS), WIDE)
    r.accp[...] = jnp.zeros((HEADS, HEADS, TILE), WIDE)
    r.accq[...] = jnp.zeros((HEADS, HEADS, TILE), WIDE)

    def step(t, at):
        at(0)
        rows = rows_at(t, TILE)
        grad = r.dot[:, rows].astype(WIDE)
        inverse = r.linv[t]
        place = iota((128, TILE), 0)
        for h in range(HEADS):
            part = slice(TILE * h, TILE * (h + 1))
            post = r.cols[:, 8 + h : 9 + h]
            w = grad * r.un[t, :, part].astype(WIDE)
            r.accp[h] += by_head(w)
            minus = -inverse[:, part] * total(post * w)
            high = minus.astype(LOW).astype(WIDE)
            r.qm[0:WIDTH, part] = (grad * post * inverse[:, part]).astype(LOW)
            extra = jnp.where(place == 0, high, jnp.where(place == 1, minus - high, 0.0))
            r.qm[WIDTH:, part] = extra.astype(LOW)
        q = r.qt[:, rows].astype(WIDE)
        for g in range(HEADS):
            r.qn[:, TILE * g : TILE * (g + 1)] = (q * r.cols[:, g : g + 1]).astype(LOW)
        for half in HALVES:
            gp = nn(r.vext[...], r.qm[:, half])
            r.gm[:, half] = (r.et[t, :, half].astype(WIDE) * gp).astype(LOW)
        r.dvt[...] += nt(r.qm[0:WIDTH, :], r.et[t])
        at(1)
        r.dkt[...] += nt(r.qn[...], r.gm[...])
        dq = jnp.zeros((WIDTH, TILE), WIDE)
        for i, half in enumerate(HALVES):
            y = nn(r.kt[...], r.gm[:, half])
            for k in range(HEADS // 2):
                g = HEADS // 2 * i + k
                part = y[:, TILE * k : TILE * (k + 1)]
                dq = dq + r.cols[:, g : g + 1] * part
                r.accq[g] += by_head(q * part)
        r.dtr[0:WIDTH, rows] = dq.astype(LOW)

    each(STEPS, TOGETHER, step, points)
    r.gsum[...] = nn(r.dot[...], r.hot[...])
    bias = r.cols[:, 16:17]
    for k in range(3):
        r.dvt[...] += (bias * r.gsum[:, k : k + 1]) * r.hott[k : k + 1, :]
    r.dtr[WIDTH : 2 * WIDTH, :] = r.dkt[...].astype(LOW)
    r.dtr[2 * WIDTH :, :] = r.dvt[...].astype(LOW)


def talking_back(r):
    lane = iota((HEADS, 128), 1)

    def lanes_sum(x):
        return jnp.sum(x, -1, keepdims=True)

    out = jnp.where(lane == 2 * HEADS, lanes_sum(by_head(r.gsum[...] * r.vsum[...])), 0.0)
    for h in range(HEADS):
        out = out + jnp.where(lane == h, lanes_sum(r.accq[h]) * DEPTH ** (-0.5), 0.0)
        out = out + jnp.where(lane == HEADS + h, lanes_sum(r.accp[h]), 0.0)
    r.late[0, :, WIDTH:] = out


def project_back_weights(r, part):
    rows = slice(128 * part, min(128 * part + 128, COLS))
    for j in range(PARTS):
        block = nn(r.dtr[COLS * j + rows.start : COLS * j + rows.stop, :], r.n1[...])
        if part == 2:
            block = jnp.concatenate([block, r.gwout[96 * j : 96 * (j + 1), :]], 0)
        block = block.T.astype(LOW).reshape(DEPS, 2, SHARD, 128)
        r.wa[j, :, :, :, 128 * part : 128 * part + 128] = block


def project_back(r):
    ones = jnp.ones((8, ROWS), LOW)
    r.late[0, 2:3, 0:WIDTH] = nt(ones, r.dtr[0:WIDTH, :])[0:1]
    r.late[0, 3:4, 0:WIDTH] = nt(ones, r.dtr[2 * WIDTH :, :])[0:1]

    def step(i, c):
        rows = rows_at(i, DENSE)
        back = nn(r.wfull[...], r.dtr[:, rows]).T
        unit, inverse = unit_of(r, 0, rows, r.patches[rows, :].astype(WIDE))
        r.late[0, 0:1, 0:WIDTH] += total(back * unit)
        r.late[0, 1:2, 0:WIDTH] += total(back)
        r.grad[rows, :] = r.grad[rows, :] + normalize_back(
            back, r.vec[0:1, :], unit, inverse
        )
        return c

    lax.fori_loop(0, ROWS // DENSE, step, 0)


MESH = pl.DeviceIdType.MESH
CHUNKS = ("a", "e", "r", "ac", "ec", "rc")
SHAPE = (PARTS, DEPS, 2, SHARD, WIDTH)
JOINED = (DEPS, 2, SHARD, PARTS * WIDTH)


class Place:
    def __init__(self, inner):
        self.inner = inner
        dp, tensor = lax.axis_index("dp"), lax.axis_index("tensor")
        self.rest = (lax.rem(dp, inner[0]), lax.rem(tensor, inner[1]))
        dp, tensor = dp // inner[0], tensor // inner[1]
        self.z, self.y = dp // 2, lax.rem(dp, 2)
        self.x, self.core = tensor // 2, lax.rem(tensor, 2)
        self.a = self.x + self.core * (self.y - self.x)
        self.b = self.y + self.core * (self.x - self.y)

    def xy(self, a, b):
        return a + self.core * (b - a), b + self.core * (a - b)

    def device(self, z, y, x, core):
        return (
            (z * 2 + y) * self.inner[0] + self.rest[0],
            (x * 2 + core) * self.inner[1] + self.rest[1],
        )

    def around(self, d):
        return lax.rem(self.z + d, DEPS)

    def z_peer(self, d):
        return self.device(self.around(d), self.y, self.x, self.core)

    def a_peer(self):
        x, y = self.xy(1 - self.a, self.b)
        return self.device(self.z, y, x, self.core)

    def b_peer(self):
        x, y = self.xy(self.a, 1 - self.b)
        return self.device(self.z, y, x, self.core)

    def x_peer(self):
        return self.device(self.z, self.y, 1 - self.x, self.core)

    def y_peer(self):
        return self.device(self.z, 1 - self.y, self.x, self.core)

    def plane_peer(self, a, b):
        x, y = self.xy(self.a + a * (1 - 2 * self.a), self.b + b * (1 - 2 * self.b))
        return self.device(self.z, y, x, self.core)

    def near(self, k):
        x = 1 - self.x if k & 4 else self.x
        y = 1 - self.y if k & 2 else self.y
        return self.device(self.z, y, x, 1 - self.core if k & 1 else self.core)

    def core_peer(self):
        return self.device(self.z, self.y, self.x, 1 - self.core)


def remote(src, dst, sems, k, device):
    return pltpu.make_async_remote_copy(
        src_ref=src,
        dst_ref=dst,
        send_sem=sems[0].at[k],
        recv_sem=sems[1].at[k],
        device_id=device,
        device_id_type=MESH,
    )


def part_of(w, j, z=slice(None), y=slice(None)):
    if len(w.shape) == 5:
        return w.at[j, z, y]
    return w.at[z, y, :, pl.ds(pl.multiple_of(j * WIDTH, 128), WIDTH)]


class Gather:
    def __init__(self, place, w, sems, base):
        self.p, self.w, self.sems, self.base = place, w, sems, base

    def copy(self, k, where, device):
        ref = part_of(self.w, *where)
        return remote(ref, ref, self.sems, self.base + k, device)

    def z_copies(self, back):
        p = self.p
        out = []
        for d in (1, 2, 3):
            z = p.around(DEPS - d) if back else p.z
            out.append(self.copy(d - 1, (p.x * 2 + p.core, z, p.y), p.z_peer(d)))
        return out

    def b_copies(self, back):
        p = self.p
        x, y = p.xy(p.a, 1 - p.b) if back else (p.x, p.y)
        return [self.copy(3, (x * 2 + p.core, slice(None), y), p.b_peer())]

    def a_copies(self, back):
        p = self.p
        a = 1 - p.a if back else p.a
        out = []
        for k, b in enumerate((p.b, 1 - p.b)):
            x, y = p.xy(a, b)
            out.append(self.copy(4 + k, (x * 2 + p.core, slice(None), y), p.a_peer()))
        return out

    def core_copies(self, back):
        p = self.p
        core = 1 - p.core if back else p.core
        return [self.copy(6 + x, (x * 2 + core,), p.core_peer()) for x in (0, 1)]

    def start(self, name):
        for copy in getattr(self, name + "_copies")(False):
            copy.start()

    def wait(self, name):
        for copy in getattr(self, name + "_copies")(True):
            copy.wait_recv()

    def drain(self):
        for name in ("z", "b", "a", "core"):
            for copy in getattr(self, name + "_copies")(False):
                copy.wait_send()


class QuickGather(Gather):
    def piece(self, a, b, back):
        p = self.p
        if back:
            a, b = p.a + a * (1 - 2 * p.a), p.b + b * (1 - 2 * p.b)
        else:
            a, b = p.a, p.b
        return p.xy(a, b)

    def plane_copy(self, q, d, back):
        p = self.p
        a, b = ((0, 1), (1, 0), (1, 1))[q]
        x, y = self.piece(a, b, back)
        where = (x * 2 + p.core, p.around(DEPS - d), y)
        return self.copy(3 + 4 * q + d, where, p.plane_peer(a, b))

    def core_copy(self, q, back):
        p = self.p
        a, b = ((0, 0), (0, 1), (1, 0), (1, 1))[q]
        x, y = self.piece(a, b, True)
        core = 1 - p.core if back else p.core
        return self.copy(15 + q, (x * 2 + core, slice(None), y), p.core_peer())

    def begin(self):
        for copy in self.z_copies(False):
            copy.start()
        for q in range(3):
            self.plane_copy(q, 0, False).start()

    def forward(self):
        for d, copy in zip((1, 2, 3), self.z_copies(True), strict=True):
            copy.wait_recv()
            for q in range(3):
                self.plane_copy(q, d, False).start()
        self.core_copy(0, False).start()

    def across(self):
        for q in range(3):
            for d in range(4):
                self.plane_copy(q, d, True).wait_recv()
            self.core_copy(1 + q, False).start()

    def end(self):
        for q in range(4):
            self.core_copy(q, True).wait_recv()

    def drain(self):
        for copy in self.z_copies(False):
            copy.wait_send()
        for q in range(3):
            for d in range(4):
                self.plane_copy(q, d, False).wait_send()
        for q in range(4):
            self.core_copy(q, False).wait_send()


class Scatter:
    def __init__(self, place, g, ins, sems, base):
        self.p, self.g, self.sems, self.base = place, g, sems, base
        self.c_in, self.a_in, self.b_in, self.z_in = ins

    def copies(self, name):
        p = self.p
        if name == "core":
            return [
                remote(part_of(self.g, x * 2 + 1 - p.core), self.c_in.at[x], self.sems, self.base + x, p.core_peer())
                for x in (0, 1)
            ]
        if name == "a":
            out = []
            for b in (0, 1):
                x, y = p.xy(1 - p.a, b)
                out.append(
                    remote(self.c_in.at[x, :, y], self.a_in.at[b], self.sems, self.base + 2 + b, p.a_peer())
                )
            return out
        if name == "b":
            return [remote(self.a_in.at[1 - p.b], self.b_in, self.sems, self.base + 4, p.b_peer())]
        return [
            remote(self.b_in.at[p.around(d)], self.z_in.at[d - 1], self.sems, self.base + 4 + d, p.z_peer(d))
            for d in (1, 2, 3)
        ]

    def start(self, name):
        for copy in self.copies(name):
            copy.start()

    def finish(self, name):
        p = self.p
        for copy in self.copies(name):
            copy.wait_recv()
        if name == "core":
            for x in (0, 1):
                self.c_in[x] += part_of(self.g, x * 2 + p.core)[...]
        elif name == "a":
            for b in (0, 1):
                x, y = p.xy(p.a, b)
                self.a_in[b] += self.c_in[x, :, y]
        elif name == "b":
            self.b_in[...] += self.a_in[p.b]

    def result(self):
        out = self.b_in[self.p.z].astype(WIDE)
        for d in range(3):
            out = out + self.z_in[d].astype(WIDE)
        return out

    def drain(self):
        for name in ("core", "a", "b", "z"):
            for copy in self.copies(name):
                copy.wait_send()


class QuickScatter(Scatter):
    def __init__(self, place, g, ins, sems, base, lane):
        super().__init__(place, g, ins, sems, base)
        self.lanes = pl.ds(lane, 128)

    def copies(self, name):
        p, base, lanes = self.p, self.base, self.lanes
        every = slice(None)
        out = []
        if name == "core":
            for x in (0, 1):
                src = self.g.at[x * 2 + 1 - p.core, :, :, :, lanes]
                dst = self.c_in.at[x, :, :, :, lanes]
                out.append(remote(src, dst, self.sems, base + x, p.core_peer()))
        elif name == "a":
            for q, (a, b) in enumerate(((0, 1), (1, 0), (1, 1))):
                x, y = p.xy(p.a + a * (1 - 2 * p.a), p.b + b * (1 - 2 * p.b))
                src = self.c_in.at[x, :, y, :, lanes]
                dst = self.a_in.at[q, :, :, lanes]
                out.append(remote(src, dst, self.sems, base + 2 + q, p.plane_peer(a, b)))
        elif name == "z":
            for d in (1, 2, 3):
                src = self.b_in.at[p.around(d), :, lanes]
                dst = self.z_in.at[d - 1, :, lanes]
                out.append(remote(src, dst, self.sems, base + 4 + d, p.z_peer(d)))
        return out

    def finish(self, name):
        p, lanes = self.p, self.lanes
        for copy in self.copies(name):
            copy.wait_recv()
        if name == "core":
            for x in (0, 1):
                self.c_in[x, :, :, :, lanes] += self.g[x * 2 + p.core, :, :, :, lanes]
        elif name == "a":
            mine = self.c_in[p.x, :, p.y, :, lanes].astype(WIDE)
            for q in range(3):
                mine = mine + self.a_in[q, :, :, lanes].astype(WIDE)
            self.b_in[:, :, lanes] = mine.astype(LOW)

    def result(self):
        out = self.b_in[self.p.z, :, self.lanes].astype(WIDE)
        for d in range(3):
            out = out + self.z_in[d, :, self.lanes].astype(WIDE)
        return out


class SlowTotal:
    def __init__(self, place, own, got, sems, base):
        self.p, self.own, self.got, self.sems, self.base = place, own, got, sems, base

    def copies(self, k):
        p = self.p
        if k < 3:
            device = (p.core_peer, p.x_peer, p.y_peer)[k]()
            return [remote(self.own.at[k], self.got.at[k], self.sems, self.base + k, device)]
        return [
            remote(self.own.at[3], self.got.at[3 + d], self.sems, self.base + 2 + d, p.z_peer(d))
            for d in (1, 2, 3)
        ]

    def start(self, k):
        for copy in self.copies(k):
            copy.start()

    def finish(self, k):
        p = self.p
        for copy in self.copies(k):
            copy.wait_recv()
        if k < 3:
            self.own[k + 1] = self.own[k] + self.got[k]
            return None
        self.got[3] = self.own[3]
        out = None
        for z in range(DEPS):
            part = self.got[3 + lax.rem(p.z - z + DEPS, DEPS)]
            out = part if z == 0 else out + part
        return out

    def drain(self):
        for k in range(4):
            for copy in self.copies(k):
                copy.wait_send()


class Total:
    def __init__(self, place, own, got, sems, base):
        self.p, self.own, self.got, self.sems, self.base = place, own, got, sems, base

    def copies(self, k):
        p = self.p
        if k == 0:
            return [
                remote(self.own.at[0], self.got.at[n], self.sems, self.base + n, p.near(n))
                for n in range(1, 8)
            ]
        return [
            remote(self.own.at[1], self.got.at[8 + d], self.sems, self.base + 7 + d, p.z_peer(d))
            for d in (1, 2, 3)
        ]

    def start(self, k):
        for copy in self.copies(k):
            copy.start()

    def finish(self, k):
        p = self.p
        for copy in self.copies(k):
            copy.wait_recv()
        self.got[8 * k] = self.own[k]
        out = None
        if k == 0:
            for n in range(8):
                x = 1 - p.x if n & 4 else p.x
                y = 1 - p.y if n & 2 else p.y
                core = 1 - p.core if n & 1 else p.core
                part = self.got[x * 4 + y * 2 + core]
                out = part if n == 0 else out + part
            self.own[1] = out
            return None
        for z in range(DEPS):
            part = self.got[8 + lax.rem(p.z - z + DEPS, DEPS)]
            out = part if z == 0 else out + part
        return out

    def drain(self):
        for k in range(2):
            for copy in self.copies(k):
                copy.wait_send()


INPUTS = ("size", "images", "patches_in", "cot_in", "classes", "class_cot")
INPUTS += ("entry", "exit", "expand", "reduce", "entry_c", "exit_c", "expand_c", "reduce_c")
INPUTS += ("vec", "talking", "off", "vec_c", "off_c")
OUTPUTS = dict(
    patch_result=((ROWS, WIDTH), LOW),
    patch_grad=((ROWS, WIDTH), WIDE),
    class_result=((3, WIDTH), LOW),
    class_grad=((3, WIDTH), WIDE),
    blocks=((6, SHARD, WIDTH), WIDE),
    rows_early=((24, WIDTH), WIDE),
    rows_late=((8, 512), WIDE),
)
COMM = {n: (SHAPE, LOW) for n in ("wa", "wa_c")}
COMM |= {n: (JOINED, LOW) for n in ("we", "wr", "we_c", "wr_c")}
COMM |= dict(
    early=((4, 24, WIDTH), WIDE),
    early_in=((7, 24, WIDTH), WIDE),
    late=((2, 8, 512), WIDE),
    late_in=((12, 8, 512), WIDE),
)
for _k in CHUNKS:
    COMM["c_in_" + _k] = ((2, DEPS, 2, SHARD, WIDTH), LOW)
    COMM["a_in_" + _k] = ((3 if _k == "a" else 2, DEPS, SHARD, WIDTH), LOW)
    COMM["b_in_" + _k] = ((DEPS, SHARD, WIDTH), LOW)
    COMM["z_in_" + _k] = ((3, SHARD, WIDTH), LOW)
SEMS = dict(g_send=59, g_recv=59, s_send=64, s_recv=64, t_send=17, t_recv=17, out=2, into=2)


def enter(p):
    barrier = pltpu.get_barrier_semaphore()
    peers = [p.z_peer(d) for d in (1, 2, 3)] + [p.near(n) for n in range(1, 8)]
    for peer in peers:
        pl.semaphore_signal(barrier, inc=1, device_id=peer, device_id_type=MESH)
    pl.semaphore_wait(barrier, len(peers))


def layer_kernel(inner, *refs):
    r = Refs(**dict(zip([*INPUTS, *OUTPUTS, *SCRATCH, *COMM, *SEMS], refs, strict=True)))
    p = Place(inner)
    mine = p.x * 2 + p.core
    weights = dict(a=r.wa, e=r.we, r=r.wr, ac=r.wa_c, ec=r.we_c, rc=r.wr_c)
    grads = weights
    first = QuickGather(p, r.wa, (r.g_send, r.g_recv), 40)
    gathers, scatters = {}, {}
    for i, k in enumerate(CHUNKS):
        if k != "a":
            gathers[k] = Gather(p, weights[k], (r.g_send, r.g_recv), 8 * (i - 1))
        ins = [getattr(r, n + "_in_" + k) for n in ("c", "a", "b", "z")]
        if k == "a":
            last = [QuickScatter(p, r.wa, ins, (r.s_send, r.s_recv), 40 + 8 * n, 128 * n) for n in range(3)]
        else:
            scatters[k] = Scatter(p, grads[k], ins, (r.s_send, r.s_recv), 8 * (i - 1))
    early = SlowTotal(p, r.early, r.early_in, (r.t_send, r.t_recv), 0)
    late = Total(p, r.late, r.late_in, (r.t_send, r.t_recv), 6)

    def go(*moves):
        def todo():
            for k, old, new in moves:
                if old:
                    gathers[k].wait(old)
                if new:
                    gathers[k].start(new)

        return todo

    def back(*moves):
        def todo():
            for k, old, new in moves:
                what = scatters.get(k) or early
                if old is not None:
                    what.finish(old)
                if new is not None:
                    what.start(new)

        return todo

    r.wa[mine, p.z, p.y] = jnp.concatenate([r.entry[...], r.exit[...]], 1)
    load = [
        pltpu.make_async_copy(r.patches_in, r.patches, r.into.at[0]),
        pltpu.make_async_copy(r.cot_in, r.cot, r.into.at[1]),
    ]
    load[0].start()
    load[1].start()
    enter(p)
    first.begin()
    part_of(r.we, mine, p.z, p.y)[...] = r.expand[...]
    part_of(r.wr, mine, p.z, p.y)[...] = r.reduce[...]
    r.wa_c[mine, p.z, p.y] = jnp.concatenate([r.entry_c[...], r.exit_c[...]], 1)
    part_of(r.we_c, mine, p.z, p.y)[...] = r.expand_c[...]
    part_of(r.wr_c, mine, p.z, p.y)[...] = r.reduce_c[...]
    columns(r)
    first.forward()
    gathers["e"].start("z")
    gathers["r"].start("z")
    masks(r)
    load[0].wait()
    norm_first(r)
    r.early[0] = jnp.zeros((24, WIDTH), WIDE)
    r.late[0] = jnp.zeros((8, 512), WIDE)
    first.across()
    first.end()
    go(("e", "z", "b"), ("ac", None, "z"))()
    project(r)
    attend(r, gather_points(go))
    gathers["e"].wait("core")
    gathers["r"].wait("core")
    feed(r, feed_points(go))
    out_result = pltpu.make_async_copy(r.result, r.patch_result, r.out.at[0])
    out_result.start()
    go(("rc", "a", "core"))()
    for k in ("ac", "ec", "rc"):
        gathers[k].wait("core")
    first.drain()
    for k in CHUNKS[1:]:
        gathers[k].drain()
    load[1].wait()
    classes(r)
    for k in ("ac", "ec", "rc"):
        scatters[k].start("core")
    feed_back(r, feed_back_points(back))
    scatters["e"].start("core")
    scatters["r"].start("core")
    attend_back(r, attend_back_points(back))
    for n in range(3):
        project_back_weights(r, n)
        last[n].start("core")
    for n in range(3):
        last[n].finish("core")
        last[n].start("a")
    talking_back(r)
    project_back(r)
    late.start(0)
    out_grad = pltpu.make_async_copy(r.grad, r.patch_grad, r.out.at[1])
    out_grad.start()
    for i, k in enumerate(CHUNKS):
        if k != "a":
            scatters[k].finish("z")
            r.blocks[i] = scatters[k].result()
    r.rows_early[...] = early.finish(3)
    last[0].finish("a")
    last[0].start("z")
    late.finish(0)
    late.start(1)
    for n in (1, 2):
        last[n].finish("a")
        last[n].start("z")
    r.rows_late[...] = late.finish(1)
    for n in range(3):
        last[n].finish("z")
        r.blocks[0, :, 128 * n : 128 * n + 128] = last[n].result()
    out_result.wait()
    out_grad.wait()
    for k in CHUNKS[1:]:
        scatters[k].drain()
    for k in last:
        k.drain()
    early.drain()
    late.drain()


def gather_points(go):
    return {
        0: go(("r", "z", "b")),
        1: go(("e", "b", "a"), ("ec", None, "z")),
        3: go(("r", "b", "a")),
        4: go(("ac", "z", "b")),
        5: go(("e", "a", "core")),
        6: go(("ac", "b", "a"), ("rc", None, "z")),
        7: go(("r", "a", "core"), ("ec", "z", "b")),
        9: go(("rc", "z", "b")),
        10: go(("ec", "b", "a"), ("ac", "a", "core")),
    }


def feed_points(go):
    return {0: go(("rc", "b", "a")), 2: go(("ec", "a", "core"))}


def feed_back_points(back):
    return {
        1: back(("ac", "core", "a")),
        2: back(("ec", "core", "a")),
    }


def attend_back_points(back):
    return {
        0: back(("ac", "a", "b"), ("rc", "core", "a")),
        1: back(("ec", "a", "b"), ("early", None, 0)),
        2: back(("e", "core", "a")),
        3: back(("rc", "a", "b"), ("ac", "b", "z")),
        4: back(("r", "core", "a"), ("ec", "b", "z"), ("early", 0, 1)),
        5: back(("e", "a", "b")),
        6: back(("rc", "b", "z")),
        7: back(("e", "b", "z"), ("early", 1, 2)),
        8: back(("r", "a", "b")),
        9: back(("early", 2, 3)),
        10: back(("r", "b", "z")),
    }


def finish_kernel(*refs):
    r = Refs(**dict(zip([*(n + "_in" for n in OUTPUTS), *FINAL], refs, strict=True)))
    r.patch_result[...] = r.patch_result_in[...]
    r.patch_grad[...] = r.patch_grad_in[...]
    r.class_result[...] = r.class_result_in[...]
    r.class_grad[...] = r.class_grad_in[...]
    for i, c in ((0, ""), (3, "_c")):
        getattr(r, "g_entry" + c)[...] = r.blocks_in[i, :, 0:COLS]
        getattr(r, "g_exit" + c)[...] = r.blocks_in[i, :, COLS:]
        getattr(r, "g_expand" + c)[...] = r.blocks_in[i + 1]
        getattr(r, "g_reduce" + c)[...] = r.blocks_in[i + 2]
    r.g_vec[0:4, :] = r.rows_late_in[0:4, 0:WIDTH]
    r.g_vec[4:10, :] = r.rows_early_in[0:6, :]
    r.g_vec_c[...] = r.rows_early_in[10:20, :]
    for j in range(PARTS):
        part = slice(WIDTH * j, WIDTH * (j + 1))
        r.g_off[part] = r.rows_early_in[6 + j : 7 + j, :].reshape(WIDTH)
        r.g_off_c[part] = r.rows_early_in[20 + j : 21 + j, :].reshape(WIDTH)
    talk = r.rows_late_in[:, WIDTH:]
    turned = jnp.concatenate([talk, jnp.zeros((120, 128), WIDE)], 0).T
    lane = iota((8, 128), 1)
    moved = pltpu.roll(turned[8:16], 8, 1)
    r.g_talking[...] = jnp.where((lane >= 8) & (lane < 16), moved, talk)[:, 0:17]


FINAL = dict(
    patch_result=((ROWS, WIDTH), LOW),
    class_result=((3, WIDTH), LOW),
    patch_grad=((ROWS, WIDTH), WIDE),
    class_grad=((3, WIDTH), WIDE),
    g_entry=((SHARD, COLS), WIDE),
    g_exit=((SHARD, 96), WIDE),
    g_expand=((SHARD, WIDTH), WIDE),
    g_reduce=((SHARD, WIDTH), WIDE),
    g_vec=((10, WIDTH), WIDE),
    g_talking=((8, 17), WIDE),
    g_off=((FF,), WIDE),
    g_entry_c=((SHARD, COLS), WIDE),
    g_exit_c=((SHARD, 96), WIDE),
    g_expand_c=((SHARD, WIDTH), WIDE),
    g_reduce_c=((SHARD, WIDTH), WIDE),
    g_vec_c=((10, WIDTH), WIDE),
    g_off_c=((FF,), WIDE),
)


def layers(inner, *args):
    smem = pl.BlockSpec(memory_space=pltpu.SMEM)
    vmem = pl.BlockSpec(memory_space=pltpu.VMEM)
    hbm = pl.BlockSpec(memory_space=pl.ANY)
    sems = [pltpu.SemaphoreType.DMA((n,)) for n in SEMS.values()]
    mid = pl.pallas_call(
        functools.partial(layer_kernel, inner),
        out_shape=[jax.ShapeDtypeStruct(*s) for s in OUTPUTS.values()],
        in_specs=[smem, smem, hbm, hbm] + [vmem] * (len(INPUTS) - 4),
        out_specs=[hbm, hbm] + [vmem] * (len(OUTPUTS) - 2),
        scratch_shapes=[pltpu.VMEM(*s) for s in (SCRATCH | COMM).values()] + sems,
        compiler_params=pltpu.CompilerParams(
            vmem_limit_bytes=63 * 2**20, collective_id=0, has_side_effects=True
        ),
    )(*args)
    out = pl.pallas_call(
        finish_kernel,
        out_shape=[jax.ShapeDtypeStruct(*s) for s in FINAL.values()],
        in_specs=[vmem] * len(OUTPUTS),
        out_specs=[vmem] * len(FINAL),
    )(*mid)
    return dict(zip(FINAL, out, strict=True))


def groups(axis, inner):
    return [[inner * k + i for i in range(inner)] for k in range(lax.axis_size(axis) // inner)]


def widen(x, inner, dims):
    for axis, n, dim in zip(("dp", "tensor"), inner, dims, strict=True):
        if n > 1:
            x = lax.all_gather(x, axis, axis=dim, tiled=True, axis_index_groups=groups(axis, n))
    return x


def narrow(x, inner, dims):
    for axis, n, dim in zip(("dp", "tensor"), inner, dims, strict=True):
        if n > 1:
            x = lax.psum_scatter(
                x, axis, scatter_dimension=dim, tiled=True, axis_index_groups=groups(axis, n)
            )
    return x


def whole(x, inner):
    for axis, n in zip(("dp", "tensor"), inner, strict=True):
        if n > 1:
            x = lax.psum(x, axis, axis_index_groups=groups(axis, n))
    return x


KINDS = ((0, 1),) * 4


def local(
    patches,
    classes,
    group_size,
    image_count,
    self_entry,
    self_exit,
    self_expand,
    self_reduce,
    self_vectors,
    self_talking,
    self_offset,
    class_entry,
    class_exit,
    class_expand,
    class_reduce,
    class_vectors,
    class_offset,
    patch_cotangent,
    class_cotangent,
):
    inner = (lax.axis_size("dp") // 8, lax.axis_size("tensor") // 4)
    weights = [
        widen(w, inner, dims)
        for w, dims in zip(
            (
                self_entry,
                self_exit,
                self_expand,
                self_reduce.T,
                class_entry,
                class_exit,
                class_expand,
                class_reduce.T,
            ),
            KINDS * 2,
            strict=True,
        )
    ]
    out = layers(
        inner,
        group_size,
        image_count,
        patches,
        patch_cotangent,
        classes,
        class_cotangent,
        *weights,
        self_vectors,
        self_talking.T,
        self_offset,
        class_vectors,
        class_offset,
    )
    names = ("entry", "exit", "expand", "reduce")
    own = [narrow(out["g_" + n], inner, dims) for n, dims in zip(names, KINDS, strict=True)]
    own_c = [narrow(out["g_" + n + "_c"], inner, dims) for n, dims in zip(names, KINDS, strict=True)]
    return (
        out["patch_result"],
        out["class_result"],
        out["patch_grad"],
        out["class_grad"],
        *own[:3],
        own[3].T,
        whole(out["g_vec"], inner),
        whole(out["g_talking"], inner).T,
        whole(out["g_off"], inner),
        *own_c[:3],
        own_c[3].T,
        whole(out["g_vec_c"], inner),
        whole(out["g_off_c"], inner),
    )


def solution(mesh):
    both = P(("dp", "tensor"), None)
    weights = (P("dp", "tensor"), P("dp", "tensor"), P("dp", "tensor"), P("tensor", "dp"))
    return jax.shard_map(
        local,
        mesh=mesh,
        in_specs=(
            both,
            both,
            P(("dp", "tensor")),
            P(("dp", "tensor")),
            *weights,
            P(),
            P(),
            P(),
            *weights,
            P(),
            P(),
            both,
            both,
        ),
        out_specs=(both, both, both, both, *weights, P(), P(), P(), *weights, P(), P()),
        check_vma=False,
    )
```

time: 1300 us -> 121 us (0.09)
  waiting for transfers between devices: 464 us -> 0 us
  matrix products: 365 us -> 0 us
  blocking collectives: 341 us -> 0 us
  Pallas kernels: 0 us -> 118 us
  other arithmetic: 69.7 us -> 0 us
  local copies, waits for them, and re-layouts: 35.1 us -> 0 us
  between operations: 17.2 us -> 2.1 us
    dot_general x49 -> x0, matrix products: 365 us -> none  [the longest x2 55 us: post_weights(): jnp.einsum('gh,hbk->gbk', mix_post, probs, precision=HIGH)]
    all_gather x14 -> x0, blocking collectives: 288 us -> none  [the longest x1 33.1 us: local(): lax.all_gather(class_expand, 'dp', axis=0, tiled=True)]
    reduce_scatter x10 -> x0, waiting for transfers between devices: 285 us -> none  [the longest x1 60 us: local(): lax.psum_scatter(class_expand_grad.astype(jnp.bfloat16), 'dp', scatter_di...]
    unnamed x20 -> x0, waiting for transfers between devices: 155 us -> none
    pallas_call x0 -> x2, Pallas kernels: none -> 118 us  [the longest x1 115 us: layers(): pl.pallas_call(functools.partial(layer_kernel, inner), out_shape=[jax.Sha...]
    psum x1 -> x0, blocking collectives: 41 us -> none  [local(): lax.psum((self_vector_grad, talking_grad, self_off_full, class_vector_gra...]
    reduce_sum x23 -> x0, other arithmetic: 30.8 us -> none  [the longest x1 15.5 us: forward_block(): total = jnp.sum(raised, -1, keepdims=True)]
    unnamed x146 -> x0, local copies, waits for them, and re-layouts: 24.7 us -> none
  transfers between devices with their start and end apart: 16 -> 0, of which waited for: 12 -> 0; matrix products, arithmetic and copies ran while one was open for 16% -> 0% of each run, Pallas kernels for 0% -> 0%
where the time goes in v1:
time: 121 us; the launch traced here: 120 us
  Pallas kernels  118 us (98%)
  between operations  2.1 us (2%)
    pallas_call x1, Pallas kernels, layers(): pl.pallas_call(functools.partial(layer_kernel, inner), out_shape=[jax.Sha...  115 us
    pallas_call x1, Pallas kernels, layers(): pl.pallas_call(finish_kernel, out_shape=[jax.ShapeDtypeStruct(*s) for s i...  3 us

profile of v1, /device:TPU:0, one launch (start us, length us, event | category | flops | bytes accessed | tf_op | source)
XLA Modules:
  0.0 120.4 jit_solution(18088299229520486436)
XLA Ops:
  2.0 115.3 %shard_map.314 = (bf16[768,384]{1,0:T(8,128)(2,1)}, f32[768,384]{1,0:T(8,128)}, bf16[3,384]{1,0:T(4,128)(2,1)}, f32[3,384]{1,0:T(4,128)}, f32[6,48,384]{2,1,0:T(...) custom-call(s32[1]{0:T(128)S(6)} %copy.36.refs_0_, s32[1]{0:T(128)S(6)} %copy.37.refs_1_, bf16[768,384]{1,0:T(8,128)(2,1)} %refs_2_.1, ...), custom_call_target="tpu_custom_call" | custom-call | tf_op jit(solution)/shard_map/pallas_call | solution.py:1199
  117.2 3.0 %shard_map.315 = (bf16[768,384]{1,0:T(8,128)(2,1)}, bf16[3,384]{1,0:T(4,128)(2,1)}, f32[768,384]{1,0:T(8,128)}, f32[3,384]{1,0:T(4,128)}, f32[48,288]{1,0:T(8,12...) custom-call(bf16[768,384]{1,0:T(8,128)(2,1)} %get-tuple-element.41.r, ...), custom_call_target="tpu_custom_call" | custom-call | tf_op jit(solution)/shard_map/pallas_call | solution.py:1209

commit v2 on v1

--- a/solution.py
+++ b/solution.py
@@ -47,6 +47,8 @@
 
 
 def rows_at(i, size):
+    if isinstance(i, int):
+        return slice(i * size, (i + 1) * size)
     return pl.ds(pl.multiple_of(i * size, size), size)
 
 
@@ -94,6 +96,8 @@
 
             def at(where):
                 for key, todo in points.items():
+                    if isinstance(key, str):
+                        continue
                     t, place = divmod(key, 2)
                     if place == where and t % together == k:
                         pl.when(i == t // together)(todo)
@@ -115,7 +119,6 @@
     patches=((ROWS, WIDTH), LOW),
     cot=((ROWS, WIDTH), LOW),
     result=((ROWS, WIDTH), LOW),
-    grad=((ROWS, WIDTH), WIDE),
     n1=((ROWS, WIDTH), LOW),
     stats=((ROWS, 128), WIDE),
     went=((3 * WIDTH, WIDTH), LOW),
@@ -133,8 +136,7 @@
     gsum=((WIDTH, 128), WIDE),
     qm=((512, SPAN), LOW),
     qn=((WIDTH, SPAN), LOW),
-    gm=((ROWS, SPAN), LOW),
-    et=((STEPS, ROWS, SPAN), LOW),
+    et=((STEPS + 1, ROWS, SPAN), LOW),
     un=((STEPS, WIDTH, SPAN), LOW),
     linv=((STEPS, 1, SPAN), WIDE),
     attt=((WIDTH, ROWS), LOW),
@@ -154,6 +156,7 @@
     d2t=((WIDTH, ROWS), LOW),
     dot=((WIDTH, ROWS), LOW),
     gwout=((WIDTH, WIDTH), WIDE),
+    sums=((8, WIDTH), WIDE),
     offset=((1, FF), WIDE),
     dvt=((WIDTH, ROWS), WIDE),
     dkt=((WIDTH, ROWS), WIDE),
@@ -248,7 +251,9 @@
     lax.fori_loop(0, ROWS // DENSE, step, 0)
     r.vsum[...] = nn(r.vt[...], r.hot[...])
     r.wback[...] = r.wout[...].T
-    r.wfull[...] = r.went[...].T
+    r.wfull[:, 0:WIDTH] = r.went[0:WIDTH, :].T
+    r.wfull[:, WIDTH : 2 * WIDTH] = r.went[2 * WIDTH :, :].T
+    r.wfull[:, 2 * WIDTH :] = r.went[WIDTH : 2 * WIDTH, :].T
 
 
 def attend(r, points):
@@ -269,10 +274,10 @@
             scores = nn(r.kext[...], r.qm[:, half])
             raised = jnp.exp(scores - jnp.max(scores, 0, keepdims=True))
             r.linv[t, :, half] = 1.0 / jnp.sum(raised, 0, keepdims=True)
-            r.et[t, :, half] = raised.astype(LOW)
+            r.et[t + 1, :, half] = raised.astype(LOW)
         at(1)
         for i, half in enumerate(HALVES):
-            mean = nn(r.vt[...], r.et[t, :, half]) * r.linv[t, :, half]
+            mean = nn(r.vt[...], r.et[t + 1, :, half]) * r.linv[t, :, half]
             r.un[t, :, half] = mean.astype(LOW)
             for k in range(HEADS // 2):
                 h = HEADS // 2 * i + k
@@ -314,9 +319,10 @@
     each(ROWS // DENSE, 1, step, points)
 
 
-def classes(r):
+def classes(r, points):
     v = lambda k: r.vec_c[k : k + 1, :]
     scale = DEPTH ** (-0.5)
+    points[0]()
     unpack_weights(r.wa_c, r.went, r.wout_c)
     wq, wk, wv = (r.went[WIDTH * k : WIDTH * (k + 1), :] for k in range(3))
     r.small8[...] = jnp.zeros((8, WIDTH), WIDE)
@@ -364,6 +370,10 @@
     middle = tokens + v(5) * branch
     normed2, unit2, inverse2 = normalize(middle, v(6), v(7))
     low2 = normed2.astype(LOW)
+    grad = r.cot8[...]
+    delta2 = (v(9) * grad).astype(LOW)
+    points[2](jnp.concatenate([low2.astype(WIDE), delta2.astype(WIDE)], 0).astype(LOW))
+    points[1]()
     expand, reduce = whole_of(r.we_c), whole_of(r.wr_c)
     hidden = nn(low2, expand) + r.off_c[...].reshape(1, FF)
     active, slope = smooth(hidden)
@@ -371,18 +381,13 @@
     branch2 = lifted + v(8)
     second = middle + v(9) * branch2
     r.class_result[...] = second[0:3].astype(LOW)
-    grad = r.cot8[...]
     grad_scale2 = total(grad * branch2)
-    delta2 = (v(9) * grad).astype(LOW)
     grad_bias2 = total(delta2.astype(WIDE))
-    low2_t, delta2_t = low2.astype(WIDE).T.astype(LOW), delta2.astype(WIDE).T.astype(LOW)
     grad_hidden = (nn(delta2, reduce) * slope.astype(WIDE)).astype(LOW)
     off = total(grad_hidden.astype(WIDE))
     for j in range(PARTS):
         r.early[0, 20 + j : 21 + j, :] = off[:, WIDTH * j : WIDTH * (j + 1)]
     back = nt(grad_hidden, expand)
-    r.we_c[...] = as_block(nn(low2_t, grad_hidden).astype(LOW))
-    r.wr_c[...] = as_block(nn(delta2_t, active).astype(LOW))
     grad_gain2, grad_shift2 = total(back * unit2), total(back)
     grad = grad + normalize_back(back, v(6), unit2, inverse2)
     grad_scale = total(grad * branch)
@@ -431,6 +436,24 @@
     )
 
 
+def class_weights(r, p):
+    rows = r.wf[...].astype(WIDE).reshape(32, 16, WIDTH)
+    normed, delta = (rows[:, k : k + 8].reshape(256, WIDTH) for k in (0, 8))
+    for k, x in enumerate((normed, delta)):
+        r.turned[k] = x.T.astype(LOW).reshape(DEPS, 2, SHARD, 256)
+    part = p.x * 2 + p.core
+    offset = r.off_c[0:WIDTH]
+    for j in range(1, PARTS):
+        offset = jnp.where(part == j, r.off_c[WIDTH * j : WIDTH * (j + 1)], offset)
+    expand = part_of(r.we_c, part)[...].reshape(WIDTH, WIDTH)
+    reduce = part_of(r.wr_c, part)[...].reshape(WIDTH, WIDTH)
+    hidden = nn(normed.astype(LOW), expand) + offset.reshape(1, WIDTH)
+    active, slope = smooth(hidden)
+    grad_hidden = (nn(delta.astype(LOW), reduce) * slope.astype(WIDE)).astype(LOW)
+    r.blocks[4] = nn(r.turned[0, p.z, p.y], grad_hidden)
+    r.blocks[5] = nn(r.turned[1, p.z, p.y], active)
+
+
 def feed_back(r, points):
     size, images = r.size[0], r.images[0]
     r.early[0, 0:10, :] = jnp.zeros((10, WIDTH), WIDE)
@@ -467,7 +490,7 @@
         add(6, back * unit)
         add(7, back)
         grad = grad + normalize_back(back, r.vec[6:7, :], unit, inverse)
-        r.grad[rows, :] = grad
+        r.middle[rows, :] = grad
         add(5, grad * r.branch1[rows, :].astype(WIDE))
         delta = (r.vec[5:6, :] * grad).astype(LOW)
         add(4, delta.astype(WIDE))
@@ -477,7 +500,10 @@
     each(ROWS // DENSE, 1, step, points)
     for half in WIDE_HALVES:
         r.we[:, :, :, half] = as_block(nn(r.n2t[...], r.slope[:, half]).astype(LOW))
+    points["expand"]()
+    for half in WIDE_HALVES:
         r.wr[:, :, :, half] = as_block(nn(r.d2t[...], r.act[:, half]).astype(LOW))
+    points["reduce"]()
     for j in range(PARTS):
         r.early[0, 6 + j : 7 + j, :] = r.offset[:, WIDTH * j : WIDTH * (j + 1)]
     r.gwout[...] = nt(r.d1t[...], r.attt[...])
@@ -485,7 +511,6 @@
 
 def attend_back(r, points):
     r.dvt[...] = jnp.zeros((WIDTH, ROWS), WIDE)
-    r.dkt[...] = jnp.zeros((WIDTH, ROWS), WIDE)
     r.accp[...] = jnp.zeros((HEADS, HEADS, TILE), WIDE)
     r.accq[...] = jnp.zeros((HEADS, HEADS, TILE), WIDE)
 
@@ -506,17 +531,14 @@
             extra = jnp.where(place == 0, high, jnp.where(place == 1, minus - high, 0.0))
             r.qm[WIDTH:, part] = extra.astype(LOW)
         q = r.qt[:, rows].astype(WIDE)
-        for g in range(HEADS):
-            r.qn[:, TILE * g : TILE * (g + 1)] = (q * r.cols[:, g : g + 1]).astype(LOW)
         for half in HALVES:
             gp = nn(r.vext[...], r.qm[:, half])
-            r.gm[:, half] = (r.et[t, :, half].astype(WIDE) * gp).astype(LOW)
-        r.dvt[...] += nt(r.qm[0:WIDTH, :], r.et[t])
+            r.et[t, :, half] = (r.et[t + 1, :, half].astype(WIDE) * gp).astype(LOW)
+        r.dvt[...] += nt(r.qm[0:WIDTH, :], r.et[t + 1])
         at(1)
-        r.dkt[...] += nt(r.qn[...], r.gm[...])
         dq = jnp.zeros((WIDTH, TILE), WIDE)
         for i, half in enumerate(HALVES):
-            y = nn(r.kt[...], r.gm[:, half])
+            y = nn(r.kt[...], r.et[t, :, half])
             for k in range(HEADS // 2):
                 g = HEADS // 2 * i + k
                 part = y[:, TILE * k : TILE * (k + 1)]
@@ -529,8 +551,20 @@
     bias = r.cols[:, 16:17]
     for k in range(3):
         r.dvt[...] += (bias * r.gsum[:, k : k + 1]) * r.hott[k : k + 1, :]
-    r.dtr[WIDTH : 2 * WIDTH, :] = r.dkt[...].astype(LOW)
-    r.dtr[2 * WIDTH :, :] = r.dvt[...].astype(LOW)
+    r.dtr[WIDTH : 2 * WIDTH, :] = r.dvt[...].astype(LOW)
+
+
+def keys_back(r, points):
+    for t in range(STEPS):
+        if t in points:
+            points[t]()
+        q = r.qt[:, rows_at(t, TILE)].astype(WIDE)
+        mixed = r.qn if t % 2 else r.qm
+        for g in range(HEADS):
+            mixed[0:WIDTH, TILE * g : TILE * (g + 1)] = (q * r.cols[:, g : g + 1]).astype(LOW)
+        part = nt(mixed[0:WIDTH, :], r.et[t])
+        r.dkt[...] = part if t == 0 else r.dkt[...] + part
+    r.dtr[2 * WIDTH :, :] = r.dkt[...].astype(LOW)
 
 
 def talking_back(r):
@@ -543,36 +577,56 @@
     for h in range(HEADS):
         out = out + jnp.where(lane == h, lanes_sum(r.accq[h]) * DEPTH ** (-0.5), 0.0)
         out = out + jnp.where(lane == HEADS + h, lanes_sum(r.accp[h]), 0.0)
-    r.late[0, :, WIDTH:] = out
-
-
-def project_back_weights(r, part):
-    rows = slice(128 * part, min(128 * part + 128, COLS))
-    for j in range(PARTS):
-        block = nn(r.dtr[COLS * j + rows.start : COLS * j + rows.stop, :], r.n1[...])
-        if part == 2:
-            block = jnp.concatenate([block, r.gwout[96 * j : 96 * (j + 1), :]], 0)
-        block = block.T.astype(LOW).reshape(DEPS, 2, SHARD, 128)
-        r.wa[j, :, :, :, 128 * part : 128 * part + 128] = block
+    r.mid[0, :, WIDTH:] = out
+
+
+def store_grads(r, j, part, rows):
+    lanes = rows.shape[0]
+    block = rows.T.astype(LOW).reshape(DEPS, 2, SHARD, lanes)
+    r.wa[j, :, :, :, 128 * part : 128 * part + lanes] = block
+
+
+def weights_early(r):
+    whole = nn(r.dtr[0 : 2 * WIDTH, :], r.n1[...])
+    query, value = whole[0:WIDTH], whole[WIDTH:]
+    gwout = r.gwout
+    store_grads(r, 0, 0, jnp.concatenate([query[0:288], gwout[0:96, :]], 0))
+    store_grads(r, 1, 0, jnp.concatenate([query[288:], gwout[96:128, :]], 0))
+    store_grads(r, 2, 0, jnp.concatenate([value[0:96], gwout[192:224, :]], 0))
+    store_grads(r, 3, 0, jnp.concatenate([value[96:], gwout[288:, :]], 0))
+
+
+def weights_late(r):
+    keys = nn(r.dtr[2 * WIDTH :, :], r.n1[...])
+    store_grads(r, 1, 1, jnp.concatenate([r.gwout[128:192, :], keys[0:192]], 0))
+    store_grads(r, 2, 1, jnp.concatenate([r.gwout[224:288, :], keys[192:]], 0))
+
+
+def project_back_start(r):
+    ones = jnp.ones((8, ROWS), LOW)
+    r.mid[0, 0:1, 0:WIDTH] = nt(ones, r.dtr[0:WIDTH, :])[0:1]
+    r.mid[0, 1:2, 0:WIDTH] = nt(ones, r.dtr[WIDTH : 2 * WIDTH, :])[0:1]
+    r.dvt[...] = nn(r.wfull[:, 0 : 2 * WIDTH], r.dtr[0 : 2 * WIDTH, :])
 
 
 def project_back(r):
-    ones = jnp.ones((8, ROWS), LOW)
-    r.late[0, 2:3, 0:WIDTH] = nt(ones, r.dtr[0:WIDTH, :])[0:1]
-    r.late[0, 3:4, 0:WIDTH] = nt(ones, r.dtr[2 * WIDTH :, :])[0:1]
+    r.sums[...] = jnp.zeros((8, WIDTH), WIDE)
 
     def step(i, c):
         rows = rows_at(i, DENSE)
-        back = nn(r.wfull[...], r.dtr[:, rows]).T
+        back = (r.dvt[:, rows] + nn(r.wfull[:, 2 * WIDTH :], r.dtr[2 * WIDTH :, rows])).T
         unit, inverse = unit_of(r, 0, rows, r.patches[rows, :].astype(WIDE))
-        r.late[0, 0:1, 0:WIDTH] += total(back * unit)
-        r.late[0, 1:2, 0:WIDTH] += total(back)
-        r.grad[rows, :] = r.grad[rows, :] + normalize_back(
+        r.sums[0:1, :] += total(back * unit)
+        r.sums[1:2, :] += total(back)
+        r.middle[rows, :] = r.middle[rows, :] + normalize_back(
             back, r.vec[0:1, :], unit, inverse
         )
         return c
 
     lax.fori_loop(0, ROWS // DENSE, step, 0)
+    for k in range(2):
+        for n in range(3):
+            r.late[0, 3 * k + n : 3 * k + n + 1, :] = r.sums[k : k + 1, 128 * n : 128 * n + 128]
 
 
 MESH = pl.DeviceIdType.MESH
@@ -860,6 +914,82 @@
         return out
 
 
+class PartScatter(QuickScatter):
+    def __init__(self, place, g, ins, sems, base, owner):
+        super().__init__(place, g, ins, sems, base, 128)
+        self.lanes = pl.ds(128, 256)
+        self.owner = owner
+
+    def core_copy(self, back):
+        p = self.p
+        x = self.owner if back else 1 - self.owner
+        src = self.g.at[x * 2 + 1 - p.core, :, :, :, self.lanes]
+        return remote(src, self.c_in.at[x, :, :, :, self.lanes], self.sems, self.base, p.core_peer())
+
+    def plane_copy(self, k):
+        p = self.p
+        y = 1 - p.y if k & 1 else p.y
+        src = self.c_in.at[self.owner, :, y, :, self.lanes]
+        dst = self.a_in.at[k - 1, :, :, self.lanes]
+        peer = (None, p.y_peer, p.x_peer, lambda: p.plane_peer(1, 1))[k]()
+        return remote(src, dst, self.sems, self.base + k, peer)
+
+    def owned(self, todo):
+        pl.when(self.p.x == self.owner)(todo)
+
+    def others(self, todo):
+        pl.when(self.p.x != self.owner)(todo)
+
+    def start(self, name):
+        if name == "core":
+            self.core_copy(False).start()
+        elif name == "a":
+            self.owned(lambda: self.plane_copy(1).start())
+
+            def both():
+                self.plane_copy(2).start()
+                self.plane_copy(3).start()
+
+            self.others(both)
+        else:
+            self.owned(lambda: QuickScatter.start(self, name))
+
+    def finish(self, name):
+        p, lanes = self.p, self.lanes
+        if name == "core":
+            self.core_copy(True).wait_recv()
+            self.c_in[self.owner, :, :, :, lanes] += self.g[self.owner * 2 + p.core, :, :, :, lanes]
+            return
+
+        def todo():
+            if name == "z":
+                QuickScatter.finish(self, name)
+                return
+            for k in (1, 2, 3):
+                self.plane_copy(k).wait_recv()
+            mine = self.c_in[self.owner, :, p.y, :, lanes].astype(WIDE)
+            for q in range(3):
+                mine = mine + self.a_in[q, :, :, lanes].astype(WIDE)
+            self.b_in[:, :, lanes] = mine.astype(LOW)
+
+        self.owned(todo)
+
+    def drain(self):
+        self.core_copy(False).wait_send()
+
+        def owned():
+            self.plane_copy(1).wait_send()
+            for copy in self.copies("z"):
+                copy.wait_send()
+
+        def others():
+            self.plane_copy(2).wait_send()
+            self.plane_copy(3).wait_send()
+
+        self.owned(owned)
+        self.others(others)
+
+
 class SlowTotal:
     def __init__(self, place, own, got, sems, base):
         self.p, self.own, self.got, self.sems, self.base = place, own, got, sems, base
@@ -954,30 +1084,35 @@
     class_grad=((3, WIDTH), WIDE),
     blocks=((6, SHARD, WIDTH), WIDE),
     rows_early=((24, WIDTH), WIDE),
-    rows_late=((8, 512), WIDE),
+    rows_mid=((8, 512), WIDE),
+    rows_late=((8, 128), WIDE),
 )
 COMM = {n: (SHAPE, LOW) for n in ("wa", "wa_c")}
 COMM |= {n: (JOINED, LOW) for n in ("we", "wr", "we_c", "wr_c")}
 COMM |= dict(
+    wf=((PARTS, DEPS, 2, 16, WIDTH), LOW),
+    turned=((2, DEPS, 2, SHARD, 256), LOW),
     early=((4, 24, WIDTH), WIDE),
     early_in=((7, 24, WIDTH), WIDE),
-    late=((2, 8, 512), WIDE),
-    late_in=((12, 8, 512), WIDE),
+    mid=((2, 8, 512), WIDE),
+    mid_in=((12, 8, 512), WIDE),
+    late=((2, 8, 128), WIDE),
+    late_in=((12, 8, 128), WIDE),
 )
-for _k in CHUNKS:
+for _k in ("a", "e", "r", "ac"):
     COMM["c_in_" + _k] = ((2, DEPS, 2, SHARD, WIDTH), LOW)
     COMM["a_in_" + _k] = ((3 if _k == "a" else 2, DEPS, SHARD, WIDTH), LOW)
     COMM["b_in_" + _k] = ((DEPS, SHARD, WIDTH), LOW)
     COMM["z_in_" + _k] = ((3, SHARD, WIDTH), LOW)
-SEMS = dict(g_send=59, g_recv=59, s_send=64, s_recv=64, t_send=17, t_recv=17, out=2, into=2)
-
-
-def enter(p):
+SEMS = dict(g_send=67, g_recv=67, s_send=64, s_recv=64, t_send=28, t_recv=28, out=2, into=2)
+
+
+def greet(p):
     barrier = pltpu.get_barrier_semaphore()
     peers = [p.z_peer(d) for d in (1, 2, 3)] + [p.near(n) for n in range(1, 8)]
     for peer in peers:
         pl.semaphore_signal(barrier, inc=1, device_id=peer, device_id_type=MESH)
-    pl.semaphore_wait(barrier, len(peers))
+    return lambda: pl.semaphore_wait(barrier, len(peers))
 
 
 def layer_kernel(inner, *refs):
@@ -991,13 +1126,22 @@
     for i, k in enumerate(CHUNKS):
         if k != "a":
             gathers[k] = Gather(p, weights[k], (r.g_send, r.g_recv), 8 * (i - 1))
+        if k in ("ec", "rc"):
+            continue
         ins = [getattr(r, n + "_in_" + k) for n in ("c", "a", "b", "z")]
         if k == "a":
-            last = [QuickScatter(p, r.wa, ins, (r.s_send, r.s_recv), 40 + 8 * n, 128 * n) for n in range(3)]
+            sems = (r.s_send, r.s_recv)
+            last = [
+                QuickScatter(p, r.wa, ins, sems, 40, 0),
+                PartScatter(p, r.wa, ins, sems, 48, p.core),
+                PartScatter(p, r.wa, ins, sems, 56, 1 - p.core),
+            ]
         else:
             scatters[k] = Scatter(p, grads[k], ins, (r.s_send, r.s_recv), 8 * (i - 1))
+    gathers["cf"] = Gather(p, r.wf, (r.g_send, r.g_recv), 59)
     early = SlowTotal(p, r.early, r.early_in, (r.t_send, r.t_recv), 0)
-    late = Total(p, r.late, r.late_in, (r.t_send, r.t_recv), 6)
+    mid = Total(p, r.mid, r.mid_in, (r.t_send, r.t_recv), 6)
+    late = Total(p, r.late, r.late_in, (r.t_send, r.t_recv), 17)
 
     def go(*moves):
         def todo():
@@ -1012,6 +1156,9 @@
     def back(*moves):
         def todo():
             for k, old, new in moves:
+                if k == "cf":
+                    go((k, old, new))()
+                    continue
                 what = scatters.get(k) or early
                 if old is not None:
                     what.finish(old)
@@ -1020,6 +1167,7 @@
 
         return todo
 
+    enter = greet(p)
     r.wa[mine, p.z, p.y] = jnp.concatenate([r.entry[...], r.exit[...]], 1)
     load = [
         pltpu.make_async_copy(r.patches_in, r.patches, r.into.at[0]),
@@ -1027,7 +1175,7 @@
     ]
     load[0].start()
     load[1].start()
-    enter(p)
+    enter()
     first.begin()
     part_of(r.we, mine, p.z, p.y)[...] = r.expand[...]
     part_of(r.wr, mine, p.z, p.y)[...] = r.reduce[...]
@@ -1036,16 +1184,16 @@
     part_of(r.wr_c, mine, p.z, p.y)[...] = r.reduce_c[...]
     columns(r)
     first.forward()
-    gathers["e"].start("z")
-    gathers["r"].start("z")
+    go(("e", None, "z"), ("r", None, "z"))()
     masks(r)
     load[0].wait()
     norm_first(r)
     r.early[0] = jnp.zeros((24, WIDTH), WIDE)
-    r.late[0] = jnp.zeros((8, 512), WIDE)
+    r.mid[0] = jnp.zeros((8, 512), WIDE)
+    r.late[0] = jnp.zeros((8, 128), WIDE)
     first.across()
     first.end()
-    go(("e", "z", "b"), ("ac", None, "z"))()
+    go(("e", "z", "b"), ("ac", None, "z"), ("ec", None, "z"), ("rc", None, "z"), ("r", "z", "b"))()
     project(r)
     attend(r, gather_points(go))
     gathers["e"].wait("core")
@@ -1053,68 +1201,83 @@
     feed(r, feed_points(go))
     out_result = pltpu.make_async_copy(r.result, r.patch_result, r.out.at[0])
     out_result.start()
-    go(("rc", "a", "core"))()
-    for k in ("ac", "ec", "rc"):
-        gathers[k].wait("core")
-    first.drain()
-    for k in CHUNKS[1:]:
-        gathers[k].drain()
-    load[1].wait()
-    classes(r)
-    for k in ("ac", "ec", "rc"):
-        scatters[k].start("core")
-    feed_back(r, feed_back_points(back))
-    scatters["e"].start("core")
-    scatters["r"].start("core")
+    def begin_class():
+        gathers["ac"].wait("core")
+        load[1].wait()
+
+    def begin_feed():
+        gathers["rc"].wait("a")
+        gathers["rc"].start("core")
+        gathers["ec"].wait("core")
+        gathers["rc"].wait("core")
+        for k in ("a", *CHUNKS[1:]):
+            (first if k == "a" else gathers[k]).drain()
+
+    def share(rows):
+        r.wf[mine, p.z, p.y] = rows
+        gathers["cf"].start("z")
+
+    classes(r, (begin_class, begin_feed, share))
+    scatters["ac"].start("core")
+    ready = {n: functools.partial(scatters[n[0]].start, "core") for n in ("expand", "reduce")}
+    feed_back(r, feed_back_points(back) | ready)
     attend_back(r, attend_back_points(back))
-    for n in range(3):
-        project_back_weights(r, n)
-        last[n].start("core")
-    for n in range(3):
-        last[n].finish("core")
-        last[n].start("a")
+    weights_early(r)
+    last[0].start("core")
+    last[1].start("core")
     talking_back(r)
+    project_back_start(r)
+    mid.start(0)
+    keys_back(r, keys_points(last, mid, back))
+    weights_late(r)
+    last[2].start("core")
     project_back(r)
+    last[2].finish("core")
+    last[2].start("a")
     late.start(0)
-    out_grad = pltpu.make_async_copy(r.grad, r.patch_grad, r.out.at[1])
+    out_grad = pltpu.make_async_copy(r.middle, r.patch_grad, r.out.at[1])
     out_grad.start()
-    for i, k in enumerate(CHUNKS):
-        if k != "a":
-            scatters[k].finish("z")
-            r.blocks[i] = scatters[k].result()
+    for n in (0, 1):
+        last[n].finish("a")
+        last[n].start("z")
+    gathers["cf"].wait("core")
+    class_weights(r, p)
+    for i, k in ((1, "e"), (2, "r"), (3, "ac")):
+        scatters[k].finish("z")
+        r.blocks[i] = scatters[k].result()
     r.rows_early[...] = early.finish(3)
-    last[0].finish("a")
-    last[0].start("z")
     late.finish(0)
     late.start(1)
-    for n in (1, 2):
-        last[n].finish("a")
-        last[n].start("z")
+    r.rows_mid[...] = mid.finish(1)
+    last[2].finish("a")
+    last[2].start("z")
     r.rows_late[...] = late.finish(1)
     for n in range(3):
         last[n].finish("z")
-        r.blocks[0, :, 128 * n : 128 * n + 128] = last[n].result()
+    r.blocks[0, :, 0:128] = last[0].result()
+    r.blocks[0, :, 128:] = last[1].result()
     out_result.wait()
     out_grad.wait()
-    for k in CHUNKS[1:]:
+    for k in ("e", "r", "ac"):
         scatters[k].drain()
+    gathers["cf"].drain()
     for k in last:
         k.drain()
     early.drain()
+    mid.drain()
     late.drain()
 
 
 def gather_points(go):
     return {
-        0: go(("r", "z", "b")),
-        1: go(("e", "b", "a"), ("ec", None, "z")),
+        0: go(("e", "b", "a")),
+        2: go(("ac", "z", "b")),
         3: go(("r", "b", "a")),
-        4: go(("ac", "z", "b")),
-        5: go(("e", "a", "core")),
-        6: go(("ac", "b", "a"), ("rc", None, "z")),
-        7: go(("r", "a", "core"), ("ec", "z", "b")),
-        9: go(("rc", "z", "b")),
-        10: go(("ec", "b", "a"), ("ac", "a", "core")),
+        5: go(("e", "a", "core"), ("ec", "z", "b")),
+        6: go(("ac", "b", "a")),
+        8: go(("r", "a", "core"), ("rc", "z", "b")),
+        9: go(("ec", "b", "a")),
+        11: go(("ac", "a", "core")),
     }
 
 
@@ -1122,48 +1285,70 @@
     return {0: go(("rc", "b", "a")), 2: go(("ec", "a", "core"))}
 
 
+def keys_points(last, mid, back):
+    def core(n):
+        def todo():
+            last[n].finish("core")
+            last[n].start("a")
+
+        return todo
+
+    def middle():
+        mid.finish(0)
+        mid.start(1)
+
+    return {0: core(0), 1: core(1), 4: middle}
+
+
 def feed_back_points(back):
     return {
-        1: back(("ac", "core", "a")),
-        2: back(("ec", "core", "a")),
+        0: back(("cf", "z", "b")),
+        2: back(("cf", "b", "a"), ("ac", "core", "a")),
     }
 
 
 def attend_back_points(back):
     return {
-        0: back(("ac", "a", "b"), ("rc", "core", "a")),
-        1: back(("ec", "a", "b"), ("early", None, 0)),
-        2: back(("e", "core", "a")),
-        3: back(("rc", "a", "b"), ("ac", "b", "z")),
-        4: back(("r", "core", "a"), ("ec", "b", "z"), ("early", 0, 1)),
-        5: back(("e", "a", "b")),
-        6: back(("rc", "b", "z")),
-        7: back(("e", "b", "z"), ("early", 1, 2)),
-        8: back(("r", "a", "b")),
-        9: back(("early", 2, 3)),
-        10: back(("r", "b", "z")),
+        0: back(("cf", "a", "core")),
+        2: back(("ac", "a", "b"), ("e", "core", "a")),
+        4: back(("r", "core", "a"), ("ac", "b", "z"), ("early", None, 0)),
+        6: back(("e", "a", "b"), ("early", 0, 1)),
+        8: back(("r", "a", "b"), ("e", "b", "z"), ("early", 1, 2)),
+        10: back(("r", "b", "z"), ("early", 2, 3)),
     }
 
 
-def finish_kernel(*refs):
+def finish_kernel(inner, *refs):
     r = Refs(**dict(zip([*(n + "_in" for n in OUTPUTS), *FINAL], refs, strict=True)))
     r.patch_result[...] = r.patch_result_in[...]
     r.patch_grad[...] = r.patch_grad_in[...]
     r.class_result[...] = r.class_result_in[...]
     r.class_grad[...] = r.class_grad_in[...]
+    r.g_entry_c[...] = r.blocks_in[3, :, 0:COLS]
+    r.g_exit_c[...] = r.blocks_in[3, :, COLS:]
+    part = lax.axis_index("tensor") // inner[1]
+    block = r.blocks_in[0]
+    one, two, three = block[:, 0:96], block[:, 96:192], block[:, 192:]
+    outer = (part == 0) | (part == 3)
+    inside = jnp.where(
+        part == 1, jnp.concatenate([one, three], 1), jnp.concatenate([three, one], 1)
+    )
+    r.g_entry[...] = jnp.where(outer, block[:, 0:COLS], inside)
+    r.g_exit[...] = jnp.where(outer, block[:, COLS:], two)
     for i, c in ((0, ""), (3, "_c")):
-        getattr(r, "g_entry" + c)[...] = r.blocks_in[i, :, 0:COLS]
-        getattr(r, "g_exit" + c)[...] = r.blocks_in[i, :, COLS:]
         getattr(r, "g_expand" + c)[...] = r.blocks_in[i + 1]
         getattr(r, "g_reduce" + c)[...] = r.blocks_in[i + 2]
-    r.g_vec[0:4, :] = r.rows_late_in[0:4, 0:WIDTH]
+    for k in range(2):
+        for n in range(3):
+            r.g_vec[k : k + 1, 128 * n : 128 * n + 128] = r.rows_late_in[3 * k + n : 3 * k + n + 1, :]
+    r.g_vec[2:4, :] = r.rows_mid_in[0:2, 0:WIDTH]
     r.g_vec[4:10, :] = r.rows_early_in[0:6, :]
     r.g_vec_c[...] = r.rows_early_in[10:20, :]
     for j in range(PARTS):
         part = slice(WIDTH * j, WIDTH * (j + 1))
         r.g_off[part] = r.rows_early_in[6 + j : 7 + j, :].reshape(WIDTH)
         r.g_off_c[part] = r.rows_early_in[20 + j : 21 + j, :].reshape(WIDTH)
-    talk = r.rows_late_in[:, WIDTH:]
+    talk = r.rows_mid_in[:, WIDTH:]
     turned = jnp.concatenate([talk, jnp.zeros((120, 128), WIDE)], 0).T
     lane = iota((8, 128), 1)
     moved = pltpu.roll(turned[8:16], 8, 1)
@@ -1207,7 +1392,7 @@
         ),
     )(*args)
     out = pl.pallas_call(
-        finish_kernel,
+        functools.partial(finish_kernel, inner),
         out_shape=[jax.ShapeDtypeStruct(*s) for s in FINAL.values()],
         in_specs=[vmem] * len(OUTPUTS),
         out_specs=[vmem] * len(FINAL),

time: 121 us -> 113 us (0.934)
  Pallas kernels: 118 us -> 111 us
    pallas_call x1, Pallas kernels: 115 us -> 108 us  [layers(): pl.pallas_call(functools.partial(layer_kernel, inner), out_shape=[jax.Sha...]
where the time goes in v2:
time: 113 us
  Pallas kernels  111 us (98%)
  between operations  2.13 us (2%)
    pallas_call x1, Pallas kernels, layers(): pl.pallas_call(functools.partial(layer_kernel, inner), out_shape=[jax.Sha...  108 us
    pallas_call x1, Pallas kernels, layers(): pl.pallas_call(functools.partial(finish_kernel, inner), out_shape=[jax.Sh...  3.1 us

profile of v2, /device:TPU:0, one launch (start us, length us, event | category | flops | bytes accessed | tf_op | source)
XLA Modules:
  0.0 113.2 jit_solution(5795127076947168022)
XLA Ops:
  2.0 108.0 %shard_map.314 = (bf16[768,384]{1,0:T(8,128)(2,1)}, f32[768,384]{1,0:T(8,128)}, bf16[3,384]{1,0:T(4,128)(2,1)}, f32[3,384]{1,0:T(4,128)}, f32[6,48,384]{2,1,0:T(...) custom-call(s32[1]{0:T(128)S(6)} %copy.36.refs_0_, s32[1]{0:T(128)S(6)} %copy.37.refs_1_, ...), custom_call_target="tpu_custom_call" | custom-call | tf_op jit(solution)/shard_map/pallas_call | solution.py:1384
  109.9 3.1 %shard_map.315 = (bf16[768,384]{1,0:T(8,128)(2,1)}, bf16[3,384]{1,0:T(4,128)(2,1)}, f32[768,384]{1,0:T(8,128)}, f32[3,384]{1,0:T(4,128)}, f32[48,288]{1,0:T(8,12...) custom-call(bf16[768,384]{1,0:T(8,128)(2,1)} %get-tuple-element.42.r, ...), custom_call_target="tpu_custom_call" | custom-call | tf_op jit(solution)/shard_map/pallas_call | solution.py:1394

commit v3 on v2

--- a/solution.py
+++ b/solution.py
@@ -353,6 +353,7 @@
     qexp = spread(queries.astype(WIDE))
     qk = (nn(qexp.astype(LOW), wk) * scale).astype(LOW)
     keys = r.next[...]
+    points[3]()
     scores = nt(qk, keys)
     size, images = r.size[0], r.images[0]
     slot = iota((PAIRS, KEYS), 0) & 7
@@ -374,9 +375,11 @@
     delta2 = (v(9) * grad).astype(LOW)
     points[2](jnp.concatenate([low2.astype(WIDE), delta2.astype(WIDE)], 0).astype(LOW))
     points[1]()
-    expand, reduce = whole_of(r.we_c), whole_of(r.wr_c)
+    expand = whole_of(r.we_c)
     hidden = nn(low2, expand) + r.off_c[...].reshape(1, FF)
     active, slope = smooth(hidden)
+    points[4]()
+    reduce = whole_of(r.wr_c)
     lifted = nt(active, reduce)
     branch2 = lifted + v(8)
     second = middle + v(9) * branch2
@@ -1205,10 +1208,14 @@
         gathers["ac"].wait("core")
         load[1].wait()
 
-    def begin_feed():
+    def begin_scores():
         gathers["rc"].wait("a")
         gathers["rc"].start("core")
+
+    def begin_feed():
         gathers["ec"].wait("core")
+
+    def begin_reduce():
         gathers["rc"].wait("core")
         for k in ("a", *CHUNKS[1:]):
             (first if k == "a" else gathers[k]).drain()
@@ -1217,7 +1224,7 @@
         r.wf[mine, p.z, p.y] = rows
         gathers["cf"].start("z")
 
-    classes(r, (begin_class, begin_feed, share))
+    classes(r, (begin_class, begin_feed, share, begin_scores, begin_reduce))
     scatters["ac"].start("core")
     ready = {n: functools.partial(scatters[n[0]].start, "core") for n in ("expand", "reduce")}
     feed_back(r, feed_back_points(back) | ready)

time: 113 us -> 112 us (level)
  no operation moved by 1% of the time
where the time goes in v3:
time: 112 us
  Pallas kernels  110 us (98%)
  between operations  2.13 us (2%)
    pallas_call x1, Pallas kernels, layers(): pl.pallas_call(functools.partial(layer_kernel, inner), out_shape=[jax.Sha...  107 us
    pallas_call x1, Pallas kernels, layers(): pl.pallas_call(functools.partial(finish_kernel, inner), out_shape=[jax.Sh...  3.1 us

profile of v3, /device:TPU:0, one launch (start us, length us, event | category | flops | bytes accessed | tf_op | source)
XLA Modules:
  0.0 112.2 jit_solution(10289931329644783857)
XLA Ops:
  2.0 107.0 %shard_map.314 = (bf16[768,384]{1,0:T(8,128)(2,1)}, f32[768,384]{1,0:T(8,128)}, bf16[3,384]{1,0:T(4,128)(2,1)}, f32[3,384]{1,0:T(4,128)}, f32[6,48,384]{2,1,0:T(...) custom-call(s32[1]{0:T(128)S(6)} %copy.36.refs_0_, s32[1]{0:T(128)S(6)} %copy.37.refs_1_, ...), custom_call_target="tpu_custom_call" | custom-call | tf_op jit(solution)/shard_map/pallas_call | solution.py:1391
  108.9 3.1 %shard_map.315 = (bf16[768,384]{1,0:T(8,128)(2,1)}, bf16[3,384]{1,0:T(4,128)(2,1)}, f32[768,384]{1,0:T(8,128)}, f32[3,384]{1,0:T(4,128)}, f32[48,288]{1,0:T(8,12...) custom-call(bf16[768,384]{1,0:T(8,128)(2,1)} %get-tuple-element.42.r, ...), custom_call_target="tpu_custom_call" | custom-call | tf_op jit(solution)/shard_map/pallas_call | solution.py:1401

commit v4 on v3

--- a/solution.py
+++ b/solution.py
@@ -28,7 +28,7 @@
 SHARD = 48
 DEPS = 4
 STEPS = ROWS // TILE
-TOGETHER = 1
+TOGETHER = 2
 KEYS = ROWS + 128
 DENSE = 384
 PAIRS = HEADS * 8
@@ -1080,6 +1080,7 @@
 INPUTS = ("size", "images", "patches_in", "cot_in", "classes", "class_cot")
 INPUTS += ("entry", "exit", "expand", "reduce", "entry_c", "exit_c", "expand_c", "reduce_c")
 INPUTS += ("vec", "talking", "off", "vec_c", "off_c")
+DIRECT = ("patches_in", "cot_in", "expand", "reduce", "expand_c", "reduce_c")
 OUTPUTS = dict(
     patch_result=((ROWS, WIDTH), LOW),
     patch_grad=((ROWS, WIDTH), WIDE),
@@ -1107,7 +1108,7 @@
     COMM["a_in_" + _k] = ((3 if _k == "a" else 2, DEPS, SHARD, WIDTH), LOW)
     COMM["b_in_" + _k] = ((DEPS, SHARD, WIDTH), LOW)
     COMM["z_in_" + _k] = ((3, SHARD, WIDTH), LOW)
-SEMS = dict(g_send=67, g_recv=67, s_send=64, s_recv=64, t_send=28, t_recv=28, out=2, into=2)
+SEMS = dict(g_send=67, g_recv=67, s_send=64, s_recv=64, t_send=28, t_recv=28, out=2, into=6)
 
 
 def greet(p):
@@ -1176,16 +1177,18 @@
         pltpu.make_async_copy(r.patches_in, r.patches, r.into.at[0]),
         pltpu.make_async_copy(r.cot_in, r.cot, r.into.at[1]),
     ]
-    load[0].start()
-    load[1].start()
+    for k, (w, src) in enumerate(
+        ((r.we, r.expand), (r.wr, r.reduce), (r.we_c, r.expand_c), (r.wr_c, r.reduce_c))
+    ):
+        load.append(pltpu.make_async_copy(src, part_of(w, mine, p.z, p.y), r.into.at[2 + k]))
+    for copy in load:
+        copy.start()
     enter()
     first.begin()
-    part_of(r.we, mine, p.z, p.y)[...] = r.expand[...]
-    part_of(r.wr, mine, p.z, p.y)[...] = r.reduce[...]
     r.wa_c[mine, p.z, p.y] = jnp.concatenate([r.entry_c[...], r.exit_c[...]], 1)
-    part_of(r.we_c, mine, p.z, p.y)[...] = r.expand_c[...]
-    part_of(r.wr_c, mine, p.z, p.y)[...] = r.reduce_c[...]
     columns(r)
+    for copy in load[2:]:
+        copy.wait()
     first.forward()
     go(("e", None, "z"), ("r", None, "z"))()
     masks(r)
@@ -1391,7 +1394,7 @@
     mid = pl.pallas_call(
         functools.partial(layer_kernel, inner),
         out_shape=[jax.ShapeDtypeStruct(*s) for s in OUTPUTS.values()],
-        in_specs=[smem, smem, hbm, hbm] + [vmem] * (len(INPUTS) - 4),
+        in_specs=[smem, smem] + [hbm if n in DIRECT else vmem for n in INPUTS[2:]],
         out_specs=[hbm, hbm] + [vmem] * (len(OUTPUTS) - 2),
         scratch_shapes=[pltpu.VMEM(*s) for s in (SCRATCH | COMM).values()] + sems,
         compiler_params=pltpu.CompilerParams(

time: 112 us -> 112 us (level)
  no operation moved by 1% of the time
where the time goes in v4:
time: 112 us
  Pallas kernels  109 us (97%)
  between operations  2.13 us (2%)
    pallas_call x1, Pallas kernels, layers(): pl.pallas_call(functools.partial(layer_kernel, inner), out_shape=[jax.Sha...  106 us
    pallas_call x1, Pallas kernels, layers(): pl.pallas_call(functools.partial(finish_kernel, inner), out_shape=[jax.Sh...  3.1 us

profile of v4, /device:TPU:0, one launch (start us, length us, event | category | flops | bytes accessed | tf_op | source)
XLA Modules:
  0.0 111.6 jit_solution(11241039754880920421)
XLA Ops:
  2.0 106.4 %shard_map.314 = (bf16[768,384]{1,0:T(8,128)(2,1)}, f32[768,384]{1,0:T(8,128)}, bf16[3,384]{1,0:T(4,128)(2,1)}, f32[3,384]{1,0:T(4,128)}, f32[6,48,384]{2,1,0:T(...) custom-call(s32[1]{0:T(128)S(6)} %copy.36.refs_0_, s32[1]{0:T(128)S(6)} %copy.37.refs_1_, ...), custom_call_target="tpu_custom_call" | custom-call | tf_op jit(solution)/shard_map/pallas_call | solution.py:1394
  108.3 3.1 %shard_map.315 = (bf16[768,384]{1,0:T(8,128)(2,1)}, bf16[3,384]{1,0:T(4,128)(2,1)}, f32[768,384]{1,0:T(8,128)}, f32[3,384]{1,0:T(4,128)}, f32[48,288]{1,0:T(8,12...) custom-call(bf16[768,384]{1,0:T(8,128)(2,1)} %get-tuple-element.42.r, ...), custom_call_target="tpu_custom_call" | custom-call | tf_op jit(solution)/shard_map/pallas_call | solution.py:1404
